TPU v7x, 32 devices: a whole 2x2x4 slice. The times are simulated.
32 devices in a mesh: sub: 8 (over z, y), split: 4 (over x, core).
Axes of the slice: x: 2, y: 2, z: 4, core: 2. Of those that a mesh axis runs over, the one named last changes fastest.
Arguments:
- stiffness: bfloat16 [8, 16, 10, 128, 128], P('sub', 'split'), may hold values from -4.2 to 4.2
- pattern: int32 [8, 16, 10], P('sub', 'split'), may hold values from 0 to 15, as said below
- mass: float32 [8, 2048], P('sub', 'split'), may hold values from 0.5 to 2
- start_modes: bfloat16 [8, 2048, 128], P('sub', 'split'), may hold values from -6 to 6
- cut_low: float32 [8], P('sub'), may hold values from 2 to 3
- cut_high: float32 [8], P('sub'), may hold values from 11 to 13
- coupling: bfloat16 [8, 8, 128, 2048], P('sub', None, None, 'split'), may hold values from -0.29882812 to 0.29882812
- incidence: int32 [8, 8], P('sub'), may hold values from 0 to 7, all different within a row
- slot_of: int32 [8], replicated, may hold values from 0 to 7, each once
Outputs:
- reduced: float32 [8, 128, 128], P('sub', 'split')
- ritz: float32 [8, 128], P('sub')
Inputs may be any that keep to these rules, and one draw needn't show every extreme that they name: pattern[s, i, 0] == i; the 10 block columns of a block row are distinct. `incidence`: each row names 8 distinct interface blocks and every interface block is named by some row. `slot_of`: a permutation.
All inputs are finite; a program needn't handle non-finite values.
Results may differ from a plain program's by a relative error of at most 0.011.
Values may be sent and summed in bfloat16 or wider, within the bound.
No kernel may reach another device: no remote copies, remote signals or barrier semaphores. Data moves between devices by JAX's collectives and lax.ppermute only.
A program may use at most 64 MiB of HBM per device.

v0:
```python
import jax
import jax.numpy as jnp
from jax import lax
from jax.sharding import PartitionSpec as P

DEG = 4
ITERS = 2


HIGH = lax.Precision.HIGHEST


def stiff_apply(stiff, pat, field):
    whole = lax.all_gather(field, "split", axis=0, tiled=True)
    block_size = stiff.shape[-1]
    blocks = whole.reshape(-1, block_size, whole.shape[1])[pat]
    prod = jnp.einsum("rkab,rkbm->ram", stiff, blocks, preferred_element_type=jnp.float32)
    return prod.reshape(-1, whole.shape[1])


def shards(stiffness, pattern, mass, start_modes, cut_low, cut_high, coupling, incidence, slot_of):
    stiff = stiffness[0]
    pat = pattern[0]
    weight = mass[0]
    phi = start_modes[0]
    kgi = coupling[0]
    links = incidence[0]
    block_size = stiff.shape[-1]
    nsplit = lax.axis_size("split")
    centre = (cut_high[0] + cut_low[0]) / 2.0
    half = (cut_high[0] - cut_low[0]) / 2.0
    for outer in range(ITERS):
        prev = phi
        image = stiff_apply(stiff, pat, phi) / weight[:, None]
        cur = ((image - centre * phi.astype(jnp.float32)) / half).astype(jnp.bfloat16)
        for inner in range(DEG - 1):
            image = stiff_apply(stiff, pat, cur) / weight[:, None]
            nxt = (
                2.0 * (image - centre * cur.astype(jnp.float32)) / half - prev.astype(jnp.float32)
            ).astype(jnp.bfloat16)
            prev, cur = (cur, nxt)
        filtered = cur.astype(jnp.float32)
        gram = lax.psum(jnp.dot((filtered * weight[:, None]).T, filtered, precision=HIGH), "split")
        lower = jnp.linalg.cholesky(gram)
        phi = lax.linalg.triangular_solve(
            lower, filtered, left_side=False, lower=True, transpose_a=True
        ).astype(jnp.bfloat16)
    local_terms = jnp.sum(phi.astype(jnp.float32) * stiff_apply(stiff, pat, phi), axis=0)
    theta = lax.psum(local_terms, "split")
    prods = jnp.einsum("ibr,rm->ibm", kgi, phi, preferred_element_type=jnp.float32)
    scaled = prods * lax.rsqrt(theta)[None, None, :]
    share = block_size // nsplit
    full = lax.psum(scaled, "split")
    own_rows = lax.dynamic_slice_in_dim(full, lax.axis_index("split") * share, share, 1)
    items = jnp.einsum("iam,ibm->iab", own_rows, full, precision=HIGH)
    faces = slot_of.shape[0]
    targets = slot_of[links]
    onehot = (targets[None, :] == jnp.arange(faces, dtype=jnp.int32)[:, None]).astype(jnp.float32)
    dense = jnp.dot(onehot, items.reshape(items.shape[0], -1), precision=HIGH).reshape(
        faces, share, block_size
    )
    owned = lax.psum_scatter(dense, "sub", scatter_dimension=0, tiled=True)
    return (owned, theta[None, :])


def solution(mesh):
    placed = (
        P("sub", "split", None, None, None),
        P("sub", "split", None),
        P("sub", "split"),
        P("sub", "split", None),
        P("sub"),
        P("sub"),
        P("sub", None, None, "split"),
        P("sub", None),
        P(),
    )
    return jax.shard_map(
        shards,
        mesh=mesh,
        in_specs=placed,
        out_specs=(P("sub", "split", None), P("sub", None)),
        check_vma=False,
    )
```

profile of v0, /device:TPU:0, one launch (start us, length us, event | category | flops | bytes accessed | tf_op | source)
XLA Modules:
  0.0 327.0 jit_solution(7024421496266153732)
XLA Ops:
  8.6 8.8 %all-gather = bf16[1,2048,128]{2,1,0:T(8,128)(2,1)S(1)} all-gather(bf16[1,512,128]{2,1,0:T(8,128)(2,1)} %param.15), channel_id=2, replica_groups=mesh['sub'=8,'split'=4] {'split'}, dimensions={1}, use_global_device_ids=true | all-gather | bytes 655360 | tf_op jit(solution)/shard_map/all_gather | solution.py:14
  17.4 1.0 copy.66
  18.5 0.7 compare_select_fusion
  19.2 0.8 gather_fusion.1
  20.1 1.2 fusion
  21.3 1.1 copy.65
  22.4 0.8 copy.72
  23.2 7.3 %all_gather.28 = bf16[2048,128]{0,1:T(8,128)(2,1)S(1)} all-gather(bf16[512,128]{0,1:T(8,128)(2,1)S(1)} %fusion.62), channel_id=1, replica_groups=mesh['sub'=8,'split'=4] {'split'}, dimensions={0}, use_global_device_ids=true | all-gather | bytes 655360 | tf_op jit(solution)/shard_map/all_gather | solution.py:14
  30.5 0.3 copy.106
  30.8 0.8 gather_fusion.2
  31.6 0.5 fusion.2
  32.3 0.5 copy-done.5
  32.8 7.3 %all_gather.29 = bf16[2048,128]{0,1:T(8,128)(2,1)S(1)} all-gather(bf16[512,128]{0,1:T(8,128)(2,1)S(1)} %fusion.68), channel_id=1, replica_groups=mesh['sub'=8,'split'=4] {'split'}, dimensions={0}, use_global_device_ids=true | all-gather | bytes 655360 | tf_op jit(solution)/shard_map/all_gather | solution.py:14
  40.1 0.3 copy.107
  40.3 0.8 gather_fusion.3
  41.2 0.5 fusion.4
  41.9 7.3 %all_gather.30 = bf16[2048,128]{0,1:T(8,128)(2,1)S(1)} all-gather(bf16[512,128]{0,1:T(8,128)(2,1)S(1)} %fusion.29), channel_id=1, replica_groups=mesh['sub'=8,'split'=4] {'split'}, dimensions={0}, use_global_device_ids=true | all-gather | bytes 655360 | tf_op jit(solution)/shard_map/all_gather | solution.py:14
  49.2 0.3 copy.108
  49.5 0.8 gather_fusion.4
  50.3 0.5 fusion.6
  50.8 0.4 copy-done.4
  51.4 1.4 convolution_bitcast_fusion.3
  53.2 31.7 %all-reduce.4.cloned.1.call-done = f32[128,128]{0,1:T(8,128)} async-done(((f32[128,128]{0,1:T(8,128)}), f32[128,128]{0,1:T(8,128)}) %all-reduce.4.cloned.1.call-update) | async-done | bytes 65552 | tf_op jit(solution)/shard_map/psum | solution.py:43
  84.9 0.9 copy.75
  85.8 0.9 fusion.81
  86.7 11.7 %cholesky.44 = f32[128,128]{1,0:T(8,128)S(1)} custom-call(f32[128,128]{1,0:T(8,128)S(1)} %fusion.81), custom_call_target="Cholesky" | custom-call | tf_op jit(solution)/shard_map/jit(cholesky)/cholesky | solution.py:44
  98.4 0.7 compare_reduce_fusion.1
  99.2 0.7 fusion.76
  99.9 9.8 %custom-call.6 = f32[1,128,128]{1,2,0:T(8,128)S(1)} custom-call(f32[1,128,128]{2,1,0:T(8,128)S(1)} %fusion.76), custom_call_target="InvertDiagBlocksLowerTriangular" | custom-call | tf_op jit(solution)/shard_map/triangular_solve/custom-call.0 | solution.py:45
  109.7 0.4 fusion.19
  110.1 6.5 %all_gather.31 = bf16[2048,128]{0,1:T(8,128)(2,1)S(1)} all-gather(bf16[512,128]{0,1:T(8,128)(2,1)S(1)} %fusion.19), channel_id=1, replica_groups=mesh['sub'=8,'split'=4] {'split'}, dimensions={0}, use_global_device_ids=true | all-gather | bytes 655360 | tf_op jit(solution)/shard_map/all_gather | solution.py:14
  116.9 0.8 gather_fusion.5
  117.7 0.5 fusion.8
  118.4 7.3 %all_gather.32 = bf16[2048,128]{0,1:T(8,128)(2,1)S(1)} all-gather(bf16[512,128]{0,1:T(8,128)(2,1)S(1)} %fusion.45), channel_id=1, replica_groups=mesh['sub'=8,'split'=4] {'split'}, dimensions={0}, use_global_device_ids=true | all-gather | bytes 655360 | tf_op jit(solution)/shard_map/all_gather | solution.py:14
  126.0 0.8 gather_fusion.6
  126.8 0.5 fusion.10
  127.8 7.3 %all_gather.33 = bf16[2048,128]{0,1:T(8,128)(2,1)S(1)} all-gather(bf16[512,128]{0,1:T(8,128)(2,1)S(1)} %fusion.46), channel_id=1, replica_groups=mesh['sub'=8,'split'=4] {'split'}, dimensions={0}, use_global_device_ids=true | all-gather | bytes 655360 | tf_op jit(solution)/shard_map/all_gather | solution.py:14
  135.1 0.3 copy.114
  135.4 0.8 gather_fusion.7
  136.2 0.5 fusion.12
  136.9 7.5 %all_gather.34 = bf16[2048,128]{0,1:T(8,128)(2,1)S(1)} all-gather(bf16[512,128]{0,1:T(8,128)(2,1)S(1)} %fusion.50), channel_id=1, replica_groups=mesh['sub'=8,'split'=4] {'split'}, dimensions={0}, use_global_device_ids=true | all-gather | bytes 655360 | tf_op jit(solution)/shard_map/all_gather | solution.py:14
  144.4 0.3 copy.116
  144.7 0.8 gather_fusion.8
  145.5 0.5 fusion.14
  146.2 0.9 fusion.24
  147.3 31.8 %all-reduce.6.cloned.1.call-done = f32[128,128]{0,1:T(8,128)} async-done(((f32[128,128]{0,1:T(8,128)}), f32[128,128]{0,1:T(8,128)}) %all-reduce.6.cloned.1.call-update) | async-done | bytes 65552 | tf_op jit(solution)/shard_map/psum | solution.py:43
  179.1 0.9 copy.86
  180.0 0.9 fusion.79
  180.9 11.7 %cholesky.55 = f32[128,128]{1,0:T(8,128)S(1)} custom-call(f32[128,128]{1,0:T(8,128)S(1)} %fusion.79), custom_call_target="Cholesky" | custom-call | tf_op jit(solution)/shard_map/jit(cholesky)/cholesky | solution.py:44
  192.6 0.6 compare_reduce_fusion
  193.3 0.7 fusion.77
  193.9 9.8 %custom-call.7 = f32[1,128,128]{1,2,0:T(8,128)S(1)} custom-call(f32[1,128,128]{2,1,0:T(8,128)S(1)} %fusion.77), custom_call_target="InvertDiagBlocksLowerTriangular" | custom-call | tf_op jit(solution)/shard_map/triangular_solve/custom-call.0 | solution.py:45
  203.7 0.4 fusion.20
  204.2 6.5 %all_gather.35 = bf16[2048,128]{0,1:T(8,128)(2,1)S(1)} all-gather(bf16[512,128]{0,1:T(8,128)(2,1)S(1)} %fusion.20), channel_id=1, replica_groups=mesh['sub'=8,'split'=4] {'split'}, dimensions={0}, use_global_device_ids=true | all-gather | bytes 655360 | tf_op jit(solution)/shard_map/all_gather | solution.py:14
  210.7 0.3 copy.118
  211.0 0.8 gather_fusion.9
  211.8 0.5 fusion.16
  212.5 6.8 %psum.30 = f32[128]{0:T(128)S(1)} all-reduce(f32[128]{0:T(128)S(1)} %multiply_reduce_fusion), channel_id=1, replica_groups=mesh['sub'=8,'split'=4] {'split'}, use_global_device_ids=true, to_apply=%region_5.8 | all-reduce | flops 128 | bytes 1024 | tf_op jit(solution)/shard_map/psum | solution.py:49
  219.3 2.5 fusion.18
  222.0 0.6 gather_fusion
  222.6 32.8 %all-reduce.8.cloned.1.call-done = f32[8,128,128]{1,2,0:T(8,128)} async-done(((f32[8,128,128]{1,2,0:T(8,128)}), f32[8,128,128]{1,2,0:T(8,128)}) %all-reduce.8.cloned.1.call-update) | async-done | bytes 524304 | tf_op jit(solution)/shard_map/psum | solution.py:53
  255.5 2.3 convolution_bitcast_fusion.2
  258.1 0.7 copy.91
  258.8 61.7 %reduce-scatter.2.cloned.1.call-done = f32[1,32,128]{2,1,0:T(8,128)} async-done(((f32[8,32,128]{2,1,0:T(8,128)}), f32[1,32,128]{2,1,0:T(8,128)}) %reduce-scatter.2.cloned.1.call-update) | async-done | bytes 16400 | tf_op jit(solution)/shard_map/reduce_scatter | solution.py:62
  (58 shorter events, 3.5 us)
Async XLA Ops:
  7.2 12.9 %copy-start = (bf16[1,4,10,128,128]{4,3,2,1,0:T(8,128)(2,1)S(1)}, bf16[1,4,10,128,128]{4,3,2,1,0:T(8,128)(2,1)}, u32[]{:S(2)}) copy-start(bf16[1,4,10,128,128]{4,3,2,1,0:T(8,128)(2,1)} %param.12) | copy-start | bytes 3932164
  7.2 77.7 %all-reduce.4.cloned.1.call-start = ((), (), s32[]{:S(2)}) async-start(), calls=%async_computation.1 | async-start | bytes 131072 | tf_op jit(solution)/shard_map/psum | solution.py:43
  20.1 3.1 copy-start.10
  32.1 0.7 copy-start.5
  41.9 7.6 %copy-start.7 = (bf16[512,128]{0,1:T(8,128)(2,1)}, bf16[512,128]{0,1:T(8,128)(2,1)S(1)}, u32[]{:S(2)}) copy-start(bf16[512,128]{0,1:T(8,128)(2,1)S(1)} %fusion.29) | copy-start | bytes 393220
  50.3 1.0 copy-start.4
  50.3 1.0 copy-start.6
  50.3 1.1 copy-start.9
  51.4 58.3 %copy-start.8 = (bf16[512,128]{0,1:T(8,128)(2,1)S(1)}, bf16[512,128]{0,1:T(8,128)(2,1)}, u32[]{:S(2)}) copy-start(bf16[512,128]{0,1:T(8,128)(2,1)} %copy-done.7) | copy-start | bytes 393220
  52.8 126.3 %all-reduce.6.cloned.1.call-start = ((), (), s32[]{:S(2)}) async-start(), calls=%async_computation.2 | async-start | bytes 131072 | tf_op jit(solution)/shard_map/psum | solution.py:43
  110.1 8.2 %copy-start.2 = (bf16[512,128]{0,1:T(8,128)(2,1)}, bf16[512,128]{0,1:T(8,128)(2,1)S(1)}, u32[]{:S(2)}) copy-start(bf16[512,128]{0,1:T(8,128)(2,1)S(1)} %fusion.19) | copy-start | bytes 393220
  126.8 0.9 copy-start.3
  147.2 108.3 %all-reduce.8.cloned.1.call-start = ((), (), s32[]{:S(2)}) async-start(), calls=%async_computation.3 | async-start | bytes 1048576 | tf_op jit(solution)/shard_map/psum | solution.py:53
  212.4 9.5 %copy-start.11 = (s32[1,8]{1,0:T(1,128)S(1)}, s32[1,8]{1,0:T(1,128)}, u32[]{:S(2)}) copy-start(s32[1,8]{1,0:T(1,128)} %param.19) | copy-start | bytes 100
  212.4 9.6 %copy-start.1 = (s32[8]{0:T(128)S(1)}, s32[8]{0:T(128)}, u32[]{:S(2)}) copy-start(s32[8]{0:T(128)} %param.20) | copy-start | bytes 100
  219.3 3.3 %copy-start.12 = (f32[128]{0:T(128)}, f32[128]{0:T(128)S(1)}, u32[]{:S(2)}) copy-start(f32[128]{0:T(128)S(1)} %psum.30) | copy-start | bytes 1540
  221.9 98.6 %reduce-scatter.2.cloned.1.call-start = ((), (), s32[]{:S(2)}) async-start(), calls=%async_computation.4 | async-start | bytes 147456 | tf_op jit(solution)/shard_map/reduce_scatter | solution.py:62
Sparse Core Ops, SparseCore 0:
  52.9 31.9 all-reduce.3
  147.3 31.7 all-reduce.5
  222.0 33.4 all-reduce.7
  259.2 61.1 reduce-scatter.1
where the time goes:
time: 328 us; the launch traced here: 327 us
  waiting for transfers between devices  158 us (48%)
  blocking collectives  72.6 us (22%)
  other arithmetic  48.9 us (15%)
  local copies, waits for them, and re-layouts  17.9 us (5%)
  between operations  15.7 us (5%)
  matrix products  13.5 us (4%)
    all_gather x9, blocking collectives, stiff_apply(): whole = lax.all_gather(field, 'split', axis=0, tiled=True)  65.8 us
    psum x2, waiting for transfers between devices, shards(): lax.psum(jnp.dot((filtered * weight[:, None]).T, filtered, precision=HIGH...  63.5 us
    reduce_scatter x1, waiting for transfers between devices, shards(): owned = lax.psum_scatter(dense, 'sub', scatter_dimension=0, tiled=True)  61.7 us
    psum x1, waiting for transfers between devices, shards(): full = lax.psum(scaled, 'split')  32.8 us
    another operation x6, other arithmetic, shards(): lower = jnp.linalg.cholesky(gram)  24.9 us
    another operation x4, other arithmetic, shards(): lax.linalg.triangular_solve(lower, filtered, left_side=False, lower=True,...  21 us
    gather x9, local copies, waits for them, and re-layouts, stiff_apply(): blocks = whole.reshape(-1, block_size, whole.shape[1])[pat]  7.22 us
    psum x1, blocking collectives, shards(): theta = lax.psum(local_terms, 'split')  6.8 us
  transfers between devices with their start and end apart: 4, of which 4 were waited for; matrix products, arithmetic and copies ran while one was open for 0% of the time, Pallas kernels for 0%

commit v1 on v0

v1 whole, which is shorter than its diff:
```python
import functools

import jax
import jax.numpy as jnp
from jax import lax
from jax.experimental import pallas as pl
from jax.experimental.pallas import tpu as pltpu
from jax.sharding import PartitionSpec as P

DEG = 4
ITERS = 2
F32 = jnp.float32
BF16 = jnp.bfloat16


def split2(x):
    hi = x.astype(BF16)
    return hi, (x - hi.astype(F32)).astype(BF16)


def inverse_factor(gram):
    n = gram.shape[0]
    lane = lax.broadcasted_iota(jnp.int32, (8, n), 1)
    sub = lax.broadcasted_iota(jnp.int32, (8, n), 0)
    groups = n // 8
    rows = [gram[8 * g : 8 * g + 8, :] for g in range(groups)]
    for j in range(n):
        gj, sj = divmod(j, 8)
        row = rows[gj][sj : sj + 1, :]
        pivot = jnp.broadcast_to(row[:, j : j + 1], (8, n))
        inv = 1.0 / pivot
        at = lane == j
        unit = jnp.where(at, 1.0, jnp.broadcast_to(row, (8, n)))
        scaled = unit * inv
        for g in range(gj, groups):
            col = jnp.broadcast_to(rows[g][:, j : j + 1], (8, n))
            if g == gj:
                if sj == 7:
                    continue
                below = sub > sj
                rows[g] = jnp.where(below, jnp.where(at, 0.0, rows[g]) - col * scaled, rows[g])
            else:
                rows[g] = jnp.where(at, 0.0, rows[g]) - col * scaled
    out = []
    for g in range(groups):
        here = lane == sub + 8 * g
        diag = jnp.sum(jnp.where(here, rows[g], 0.0), axis=1, keepdims=True)
        lower = jnp.where(lane < sub + 8 * g, rows[g], jnp.where(here, 1.0, 0.0))
        out.append(lower * lax.rsqrt(diag))
    return jnp.concatenate(out, axis=0).T


def filter_kernel(nranks, pat, rank, ends, mass, k0, k1, k2, k3, y0, y1, y2, y3, phi_out, theta_out, stiff, ya, yb, scale, ksem, ysem):
    nb, nzb = pat.shape
    bs = stiff.shape[-1]
    own = nb // nranks
    me = rank[0]
    copies = []
    for t, ref in enumerate((y0, y1, y2, y3)):
        at = pl.multiple_of((me ^ t) * (own * bs), own * bs)
        copies.append(pltpu.make_async_copy(ref, ya.at[pl.ds(at, own * bs)], ysem.at[t]))
        copies[-1].start()
    kcopies = []
    for t, ref in enumerate((k0, k1, k2, k3)):
        kcopies.append(pltpu.make_async_copy(ref, stiff.at[pl.ds((me ^ t) * own, own)], ksem.at[t]))
        kcopies[-1].start()
    centre = (ends[1] + ends[0]) / 2.0
    half = (ends[1] - ends[0]) / 2.0
    for i in range(nb):
        row = jnp.broadcast_to(mass[i : i + 1, :], (bs, bs)).T
        scale[i * bs : (i + 1) * bs, :] = 1.0 / (row * half)
    shift = jnp.full((1, 1), centre, F32) / half
    for c in copies:
        c.wait()

    def image(i, src):
        left = jnp.concatenate([stiff[i, k] for k in range(nzb)], axis=1)
        right = jnp.concatenate(
            [src[pl.ds(pl.multiple_of(pat[i, k] * bs, bs), bs), :] for k in range(nzb)], axis=0
        )
        return jnp.dot(left, right, preferred_element_type=F32)

    def rows_of(i):
        return pl.ds(pl.multiple_of(i * bs, bs), bs)

    def first(i):
        at = rows_of(i)
        yb[at, :] = (image(i, ya) * scale[at, :] - shift * ya[at, :].astype(F32)).astype(BF16)

    def later(i, src, dst):
        at = rows_of(i)
        dst[at, :] = (
            2.0 * (image(i, src) * scale[at, :] - shift * src[at, :].astype(F32)) - dst[at, :].astype(F32)
        ).astype(BF16)

    step = 2

    def sweep(body):
        @pl.loop(0, nb, step=step)
        def _(i):
            for u in range(step):
                body(i + u)

    def finish():
        src, dst = yb, ya
        for _ in range(DEG - 1):
            sweep(lambda i, src=src, dst=dst: later(i, src, dst))
            src, dst = dst, src
        cur = src
        gram = jnp.zeros((bs, bs), F32)
        for i in range(nb):
            blk = cur[i * bs : (i + 1) * bs, :]
            row = jnp.broadcast_to(mass[i : i + 1, :], (bs, bs)).T
            hi, lo = split2(blk.astype(F32) * row)
            both = lax.dot_general(
                blk, jnp.concatenate([hi, lo], axis=1), (((0,), (0,)), ((), ())), preferred_element_type=F32
            )
            gram = gram + both[:, :bs] + both[:, bs:]
        hi, lo = split2(inverse_factor(gram))
        weights = jnp.concatenate([hi, lo], axis=0)
        for i in range(nb):
            blk = cur[i * bs : (i + 1) * bs, :]
            ya[i * bs : (i + 1) * bs, :] = jnp.dot(
                jnp.concatenate([blk, blk], axis=1), weights, preferred_element_type=F32
            ).astype(BF16)

    @pl.loop(0, ITERS)
    def _(it):
        for t in range(nranks):

            @pl.when(it == 0)
            def _(t=t):
                kcopies[t].wait()

            base = (me ^ t) * own
            for r in range(own):
                first(base + r)
        finish()

    theta_out[...] = jnp.zeros_like(theta_out)

    @pl.loop(0, nb, step=step)
    def _(i):
        for u in range(step):
            at = rows_of(i + u)
            prod = ya[at, :].astype(F32) * image(i + u, ya)
            theta_out[...] += jnp.sum(prod, axis=0, keepdims=True)

    phi_out[...] = ya[...]


def face_kernel(nranks, rank, targets, theta, phi, c0, c1, c2, c3, keep, send):
    me = rank[0]
    njs, bs, cols = c0.shape
    faces, share = keep.shape[0], keep.shape[1]
    keep[...] = jnp.zeros_like(keep)
    send[...] = jnp.zeros_like(send)
    rs = lax.rsqrt(theta[...])
    for j in range(njs):
        prod = jnp.zeros((bs, bs), F32)
        for t, ref in enumerate((c0, c1, c2, c3)):
            at = pl.multiple_of((me ^ t) * cols, cols)
            prod = prod + jnp.dot(ref[j], phi[pl.ds(at, cols), :], preferred_element_type=F32)
        hi, lo = split2(prod * rs)
        left = jnp.concatenate([hi, lo, hi], axis=1)
        right = jnp.concatenate([hi, hi, lo], axis=1)
        item = lax.dot_general(left, right, (((1,), (1,)), ((), ())), preferred_element_type=F32)
        pieces = [item[share * r : share * (r + 1), :] for r in range(nranks)]
        mine = pieces[0]
        other = pieces[0]
        for r in range(1, nranks):
            mine = jnp.where(me == r, pieces[r], mine)
            other = jnp.where((me ^ 1) == r, pieces[r], other)
        keep[targets[j]] = mine
        send[targets[j]] = other.astype(BF16)


def shards(stiffness, pattern, mass, start_modes, cut_low, cut_high, coupling, incidence, slot_of):
    stiff = stiffness[0]
    own, nzb, bs, _ = stiff.shape
    modes = start_modes.shape[-1]
    nranks = lax.axis_size("split")
    nsub = lax.axis_size("sub")
    me = lax.axis_index("split")
    sub = lax.axis_index("sub")
    nb = own * nranks
    faces = slot_of.shape[0]
    nif = coupling.shape[1]
    assert nranks == 4 and nsub & (nsub - 1) == 0

    def swap(x, bits, axis="split", n=nranks):
        return lax.ppermute(x, axis, [(i, i ^ bits) for i in range(n)])

    y_x = swap(start_modes[0], 2)
    small = jnp.concatenate(
        [mass[0].reshape(-1, 128), jnp.pad(pattern[0].astype(F32).reshape(1, -1), ((0, 0), (0, 128 - own * nzb)))], axis=0
    )
    s_x = swap(small, 2)
    k_x = swap(stiff, 2)
    y_c = swap(start_modes[0], 1)
    s_c = swap(small, 1)
    k_c = swap(stiff, 1)
    s_d = swap(s_x, 1)
    y_d = swap(y_x, 1)
    k_d = swap(k_x, 1)

    halfj = nif // 2
    parity = me % 2
    coup = coupling[0]
    same = lax.dynamic_slice_in_dim(coup, parity * halfj, halfj, 0)
    other = lax.dynamic_slice_in_dim(coup, (1 - parity) * halfj, halfj, 0)
    g_x = swap(same, 2)
    g_d = swap(other, 3)
    g_c = swap(other, 1)

    smalls = jnp.stack([small, s_c, s_x, s_d])[jnp.arange(nranks) ^ me]
    mass_all = smalls[:, :-1].reshape(nb, bs)
    pat_all = smalls[:, -1, : own * nzb].astype(jnp.int32).reshape(nb, nzb)
    ends = jnp.concatenate([cut_low, cut_high])
    rank = me.astype(jnp.int32).reshape(1)

    smem = pl.BlockSpec(memory_space=pltpu.SMEM)
    vmem = pl.BlockSpec(memory_space=pltpu.VMEM)
    hbm = pl.BlockSpec(memory_space=pl.ANY)
    phi, theta = pl.pallas_call(
        functools.partial(filter_kernel, nranks),
        out_shape=(
            jax.ShapeDtypeStruct((nb * bs, modes), BF16),
            jax.ShapeDtypeStruct((1, modes), F32),
        ),
        in_specs=[smem, smem, smem, vmem] + [hbm] * 8,
        out_specs=(vmem, vmem),
        scratch_shapes=[
            pltpu.VMEM((nb, nzb, bs, bs), BF16),
            pltpu.VMEM((nb * bs, modes), BF16),
            pltpu.VMEM((nb * bs, modes), BF16),
            pltpu.VMEM((nb * bs, modes), F32),
            pltpu.SemaphoreType.DMA((4,)),
            pltpu.SemaphoreType.DMA((4,)),
        ],
        compiler_params=pltpu.CompilerParams(vmem_limit_bytes=40 << 20),
        name="filter",
    )(pat_all, rank, ends, mass_all, stiff, k_c, k_x, k_d, start_modes[0], y_c, y_x, y_d)

    links = lax.dynamic_slice_in_dim(incidence[0], parity * halfj, halfj, 0)
    targets = slot_of[links] ^ (sub * (faces // nsub))
    share = bs // nranks
    keep, send = pl.pallas_call(
        functools.partial(face_kernel, nranks),
        out_shape=(
            jax.ShapeDtypeStruct((faces, share, bs), F32),
            jax.ShapeDtypeStruct((faces, share, bs), BF16),
        ),
        in_specs=[smem, smem, vmem, vmem] + [vmem] * 4,
        out_specs=(vmem, vmem),
        compiler_params=pltpu.CompilerParams(vmem_limit_bytes=40 << 20),
        name="faces",
    )(rank, targets, theta, phi, same, g_c, g_x, g_d)
    total = keep + swap(send, 1).astype(F32)
    width = nsub // 2
    per = faces // nsub
    while width:
        lo, hi = total[: width * per], total[width * per :]
        total = lo + swap(hi.astype(BF16), width, "sub", nsub).astype(F32)
        width //= 2
    return (total, theta)


def solution(mesh):
    placed = (
        P("sub", "split", None, None, None),
        P("sub", "split", None),
        P("sub", "split"),
        P("sub", "split", None),
        P("sub"),
        P("sub"),
        P("sub", None, None, "split"),
        P("sub", None),
        P(),
    )
    return jax.shard_map(
        shards,
        mesh=mesh,
        in_specs=placed,
        out_specs=(P("sub", "split", None), P("sub", None)),
        check_vma=False,
    )
```

time: 328 us -> 137 us (0.42)
  waiting for transfers between devices: 158 us -> 40.6 us
  blocking collectives: 72.6 us -> 0 us
  Pallas kernels: 0 us -> 65 us
  other arithmetic: 48.9 us -> 6.01 us
  between operations: 15.7 us -> 2.11 us
  matrix products: 13.5 us -> 0 us
  starting transfers between devices: 0.34 us -> 13.7 us
  local copies, waits for them, and re-layouts: 17.9 us -> 8.74 us
    psum x3 -> x0, waiting for transfers between devices: 96.4 us -> none  [the longest x2 63.5 us: shards(): lax.psum(jnp.dot((filtered * weight[:, None]).T, filtered, precision=HIGH...]
    all_gather x9 -> x0, blocking collectives: 65.8 us -> none  [stiff_apply(): whole = lax.all_gather(field, 'split', axis=0, tiled=True)]
    pallas_call x0 -> x2, Pallas kernels: none -> 65 us  [the longest x1 62.2 us: shards(): pl.pallas_call(functools.partial(filter_kernel, nranks), out_shape=(jax.S...]
    reduce_scatter x1 -> x0, waiting for transfers between devices: 61.7 us -> none  [shards(): owned = lax.psum_scatter(dense, 'sub', scatter_dimension=0, tiled=True)]
    another operation x10 -> x2, other arithmetic: 45.8 us -> 2.02 us  [shards(): smalls = jnp.stack([small, s_c, s_x, s_d])[jnp.arange(nranks) ^ me]]
    ppermute x0 -> x16, waiting for transfers between devices: none -> 40.6 us  [swap(): return lax.ppermute(x, axis, [(i, i ^ bits) for i in range(n)])]
    ppermute x0 -> x16, starting transfers between devices: none -> 13.7 us  [swap(): return lax.ppermute(x, axis, [(i, i ^ bits) for i in range(n)])]
    dot_general x14 -> x0, matrix products: 12.6 us -> none  [the longest x9 5.13 us: stiff_apply(): jnp.einsum('rkab,rkbm->ram', stiff, blocks, preferred_element_type=jnp.fl...]
  transfers between devices with their start and end apart: 4 -> 16, of which waited for: 4 -> 6; matrix products, arithmetic and copies ran while one was open for 0% -> 9% of each run, Pallas kernels for 0% -> 46%
where the time goes in v1:
time: 137 us; the launch traced here: 136 us
  Pallas kernels  65 us (47%)
  waiting for transfers between devices  40.6 us (30%)
  starting transfers between devices  13.7 us (10%)
  local copies, waits for them, and re-layouts  8.74 us (6%)
  other arithmetic  6.01 us (4%)
  between operations  2.11 us (2%)
    pallas_call x1, Pallas kernels, shards(): pl.pallas_call(functools.partial(filter_kernel, nranks), out_shape=(jax.S...  62.2 us
    ppermute x16, waiting for transfers between devices, swap(): return lax.ppermute(x, axis, [(i, i ^ bits) for i in range(n)])  40.6 us
    ppermute x16, starting transfers between devices, swap(): return lax.ppermute(x, axis, [(i, i ^ bits) for i in range(n)])  13.7 us
    pallas_call x1, Pallas kernels, shards(): pl.pallas_call(functools.partial(face_kernel, nranks), out_shape=(jax.Sha...  2.79 us
  transfers between devices with their start and end apart: 16, of which 6 were waited for; matrix products, arithmetic and copies ran while one was open for 9% of the time, Pallas kernels for 46%

profile of v1, /device:TPU:0, one launch (start us, length us, event | category | flops | bytes accessed | tf_op | source)
XLA Modules:
  0.0 136.2 jit_solution(9610000887698649091)
XLA Ops:
  0.6 0.0 copy-start
  0.6 0.0 copy-start.2
  0.7 0.0 copy-start.6
  0.7 3.0 %collective-permute-start.4 = (bf16[4,10,128,128]{3,2,1,0:T(8,128)(2,1)}, bf16[4,10,128,128]{3,2,1,0:T(8,128)(2,1)S(1)}, u32[]{:S(2)}, u32[]{:S(2)}) collective-permute-start(bf16[4,10,128,128]{3,2,1,0:T(8,128)(2,1)} %bitcast.24), channel_id=1, source_target_pairs={{0,2},{1,3},{2,0},{3,1},{4,6},{5,7},{6,4},{7,5},{8,10},{9,11},{10,... | collective-permute-start | bytes 3932168 | tf_op jit(solution)/shard_map/ppermute | solution.py:192
  3.7 0.0 collective-permute-start.3
  3.7 29.0 %collective-permute-done.4.k2 = bf16[4,10,128,128]{3,2,1,0:T(8,128)(2,1)S(1)} collective-permute-done((bf16[4,10,128,128]{3,2,1,0:T(8,128)(2,1)}, bf16[4,10,128,128]{3,2,1,0:T(8,128)(2,1)S(1)}, u32[]{:S(2)}, u32[]{:S(2)}) %collective-permute-start.4) | collective-permute-done | bytes 1310752 | tf_op jit(solution)/shard_map/ppermute | solution.py:192
  32.7 0.0 collective-permute-start.5
  32.7 0.7 convert_element_type.37
  33.3 0.1 convert_element_type.38
  33.4 0.7 fusion.4
  34.1 1.7 %collective-permute-start.1 = (f32[5,128]{1,0:T(8,128)S(1)}, f32[5,128]{1,0:T(8,128)}, u32[]{:S(2)}, u32[]{:S(2)}) collective-permute-start(f32[5,128]{1,0:T(8,128)S(1)} %get-tuple-element.13), channel_id=1, source_target_pairs={{0,2},{1,3},{2,0},{3,1},{4,6},{5,7},{6,4},{7,5},{8,10},{9,11},{10,... | collective-permute-start | bytes 7688 | tf_op jit(solution)/shard_map/ppermute | solution.py:192
  35.9 0.2 collective-permute-start
  36.1 0.4 collective-permute-start.7
  36.4 0.0 copy-start.1
  36.4 2.2 %dynamic-slice_bitcast_fusion = (bf16[4,128,512]{2,1,0:T(8,128)(2,1)}, bf16[4,128,512]{2,1,0:T(8,128)(2,1)S(1)}) fusion(bf16[1,8,128,512]{3,2,1,0:T(8,128)(2,1)} %param.15, s32[]{:T(128)S(6)} %select_n.38, s32[]{:T(128)S(6)} %select_n.35), kind=kLoop, calls=%fused_computation.2 | loop fusion | bytes 2097160 | tf_op jit(solution)/shard_map/dynamic_slice | solution.py:211
  38.6 0.0 copy-done.6
  38.6 0.1 fusion.3
  38.7 0.0 collective-permute-done.1
  38.7 0.0 copy-done.2
  38.7 0.1 collective-permute-start.6
  38.8 3.2 %collective-permute-done.7.y2 = bf16[512,128]{1,0:T(8,128)(2,1)S(1)} collective-permute-done((bf16[512,128]{1,0:T(8,128)(2,1)}, bf16[512,128]{1,0:T(8,128)(2,1)S(1)}, u32[]{:S(2)}, u32[]{:S(2)}) %collective-permute-start.7) | collective-permute-done | bytes 131104 | tf_op jit(solution)/shard_map/ppermute | solution.py:192
  42.0 0.0 collective-permute-start.8
  42.0 0.0 collective-permute-done
  42.0 0.6 collective-permute-start.2
  43.9 0.0 copy-done
  43.9 1.1 gather_fusion
  45.0 0.0 collective-permute-done.2
  45.0 0.0 collective-permute-start.9
  45.1 0.0 collective-permute-done.6.y1
  45.1 0.4 collective-permute-start.11
  45.4 0.0 collective-permute-done.8.y3
  45.4 1.7 %collective-permute-start.10 = (bf16[4,128,512]{2,1,0:T(8,128)(2,1)S(1)}, bf16[4,128,512]{2,1,0:T(8,128)(2,1)}, u32[]{:S(2)}, u32[]{:S(2)}) collective-permute-start(bf16[4,128,512]{2,1,0:T(8,128)(2,1)S(1)} %get-tuple-element.11.c0), channel_id=1, source_target_pairs={{0,2},{1,3},{2,0},{3,1},{4,6},{5,7},{6,4},{7,5},{8,10},{9,11},{10,... | collective-permute-start | bytes 1572872 | tf_op jit(solution)/shard_map/ppermute | solution.py:192
  47.2 0.1 pad_maximum_fusion.1.ends
  47.3 1.2 broadcast_xor_fusion.targets
  48.4 1.3 pad_maximum_fusion
  49.8 1.9 %gather_fusion.1 = f32[4,5,128]{2,1,0:T(8,128)} fusion(f32[4,5,128]{2,1,0:T(8,128)} %pad_maximum_fusion, s32[1024]{0:T(1024)S(1)} %pad_clamp_fusion), kind=kCustom, calls=%fused_computation.1 | custom fusion | bytes 20496 | tf_op jit(solution)/shard_map/gather | solution.py:216
  51.6 1.3 slice.40
  52.9 1.3 fusion
  54.3 0.7 convert_element_type.40.pat
  55.0 0.0 collective-permute-done.3.k1
  55.0 0.0 collective-permute-done.5.k3
  55.0 0.0 copy-done.1
  55.0 0.0 copy-start.3
  55.0 0.7 copy-done.3
  55.7 0.0 copy-start.5
  55.7 62.2 %filter.1 = (bf16[2048,128]{1,0:T(8,128)(2,1)S(1)}, f32[1,128]{1,0:T(1,128)}) custom-call(s32[16,10]{1,0:T(8,128)S(1)} %convert_element_type.40.pat, s32[1]{0:T(128)} %bitcast.rank, f32[2]{0:T(128)S(1)} %pad_maximum_fusion.1.ends, f32[16,128]{1,0:T(8,128)S(1)} %bitcast.30, bf16[4,10,128,128]{3,2,1,0:T(8,128)(2,1)S(1)} %bitcast.26, ...), custom_call_target="tpu_custom_call" | custom-call | tf_op jit(solution)/shard_map/filter/pallas_call | solution.py:225
  117.9 0.0 collective-permute-done.9.c1
  117.9 0.0 collective-permute-done.10.c2
  118.0 0.0 collective-permute-done.11.c3
  118.0 0.0 copy-done.5
  118.0 0.0 copy-start.4
  118.0 0.6 copy-done.4
  118.6 2.8 %faces.1 = (f32[8,32,128]{2,1,0:T(8,128)S(1)}, bf16[8,32,128]{2,1,0:T(8,128)(2,1)S(1)}) custom-call(s32[1]{0:T(128)} %bitcast.rank, s32[4]{0:T(128)S(1)} %copy-done.5, f32[1,128]{1,0:T(1,128)S(1)} %copy-done.4, bf16[2048,128]{1,0:T(8,128)(2,1)S(1)} %get-tuple-element.7.phi, bf16[4,128,512]{2,1,0:T(8,128)(2,1)S(1)} %get-tuple-element.11.c0, ...), custom_call_target="tpu_custom_call" | custom-call | tf_op jit(solution)/shard_map/faces/pallas_call | solution.py:248
  121.4 0.1 collective-permute-start.12
  121.5 1.2 collective-permute-done.12
  122.8 2.6 %collective-permute-start.13 = (bf16[4,32,128]{2,1,0:T(8,128)(2,1)S(1)}, bf16[4,32,128]{2,1,0:T(8,128)(2,1)S(1)}, u32[]{:S(2)}, u32[]{:S(2)}) collective-permute-start(bf16[4,32,128]{2,1,0:T(8,128)(2,1)S(1)} %slice.56), channel_id=1, source_target_pairs={{0,16},{4,20},{8,24},{12,28},{16,0},{20,4},{24,8},{28,12},{1,17},{... | collective-permute-start | bytes 98312 | tf_op jit(solution)/shard_map/ppermute | solution.py:192
  125.4 2.6 %collective-permute-done.13 = bf16[4,32,128]{2,1,0:T(8,128)(2,1)S(1)} collective-permute-done((bf16[4,32,128]{2,1,0:T(8,128)(2,1)S(1)}, bf16[4,32,128]{2,1,0:T(8,128)(2,1)S(1)}, u32[]{:S(2)}, u32[]{:S(2)}) %collective-permute-start.13) | collective-permute-done | bytes 32800 | tf_op jit(solution)/shard_map/ppermute | solution.py:192
  128.0 1.3 collective-permute-start.14
  129.3 2.5 %collective-permute-done.14 = bf16[2,32,128]{2,1,0:T(8,128)(2,1)S(1)} collective-permute-done((bf16[2,32,128]{2,1,0:T(8,128)(2,1)S(1)}, bf16[2,32,128]{2,1,0:T(8,128)(2,1)S(1)}, u32[]{:S(2)}, u32[]{:S(2)}) %collective-permute-start.14) | collective-permute-done | bytes 16416 | tf_op jit(solution)/shard_map/ppermute | solution.py:192
  131.9 1.6 %collective-permute-start.15 = (bf16[1,32,128]{2,1,0:T(8,128)(2,1)S(1)}, bf16[1,32,128]{2,1,0:T(8,128)(2,1)S(1)}, u32[]{:S(2)}, u32[]{:S(2)}) collective-permute-start(bf16[1,32,128]{2,1,0:T(8,128)(2,1)S(1)} %slice.58), channel_id=1, source_target_pairs={{0,4},{4,0},{8,12},{12,8},{16,20},{20,16},{24,28},{28,24},{1,5},{5... | collective-permute-start | bytes 24584 | tf_op jit(solution)/shard_map/ppermute | solution.py:192
  133.4 2.1 %collective-permute-done.15 = bf16[1,32,128]{2,1,0:T(8,128)(2,1)S(1)} collective-permute-done((bf16[1,32,128]{2,1,0:T(8,128)(2,1)S(1)}, bf16[1,32,128]{2,1,0:T(8,128)(2,1)S(1)}, u32[]{:S(2)}, u32[]{:S(2)}) %collective-permute-start.15) | collective-permute-done | bytes 8224 | tf_op jit(solution)/shard_map/ppermute | solution.py:192
  135.6 0.6 slice_add_fusion.2
  (9 shorter events, 0.1 us)
Async XLA Ops:
  0.6 43.2 %copy-start = (s32[8]{0:T(128)S(1)}, s32[8]{0:T(128)}, u32[]{:S(2)}) copy-start(s32[8]{0:T(128)} %param.17) | copy-start | bytes 100
  0.6 38.1 %copy-start.2 = (bf16[1,512,128]{2,1,0:T(8,128)(2,1)S(1)}, bf16[1,512,128]{2,1,0:T(8,128)(2,1)}, u32[]{:S(2)}) copy-start(bf16[1,512,128]{2,1,0:T(8,128)(2,1)} %param.12) | copy-start | bytes 393220
  0.7 38.0 %copy-start.6 = (s32[1,8]{1,0:T(1,128)S(1)}, s32[1,8]{1,0:T(1,128)}, u32[]{:S(2)}) copy-start(s32[1,8]{1,0:T(1,128)} %param.16) | copy-start | bytes 100
  0.7 32.0 %collective-permute-start.4 = (bf16[4,10,128,128]{3,2,1,0:T(8,128)(2,1)}, bf16[4,10,128,128]{3,2,1,0:T(8,128)(2,1)S(1)}, u32[]{:S(2)}, u32[]{:S(2)}) collective-permute-start(bf16[4,10,128,128]{3,2,1,0:T(8,128)(2,1)} %bitcast.24), channel_id=1, source_target_pairs={{0,2},{1,3},{2,0},{3,1},{4,6},{5,7},{6,4},{7,5},{8,10},{9,11},{10,... | collective-permute-start | bytes 3932168 | tf_op jit(solution)/shard_map/ppermute | solution.py:192
  3.7 51.3 %collective-permute-start.3 = (bf16[4,10,128,128]{3,2,1,0:T(8,128)(2,1)}, bf16[4,10,128,128]{3,2,1,0:T(8,128)(2,1)}, u32[]{:S(2)}, u32[]{:S(2)}) collective-permute-start(bf16[4,10,128,128]{3,2,1,0:T(8,128)(2,1)} %bitcast.25), channel_id=1, source_target_pairs={{0,1},{1,0},{2,3},{3,2},{4,5},{5,4},{6,7},{7,6},{8,9},{9,8},{10,11... | collective-permute-start | bytes 3932168 | tf_op jit(solution)/shard_map/ppermute | solution.py:192
  32.7 22.4 %collective-permute-start.5 = (bf16[4,10,128,128]{3,2,1,0:T(8,128)(2,1)S(1)}, bf16[4,10,128,128]{3,2,1,0:T(8,128)(2,1)}, u32[]{:S(2)}, u32[]{:S(2)}) collective-permute-start(bf16[4,10,128,128]{3,2,1,0:T(8,128)(2,1)S(1)} %collective-permute-done.4.k2), channel_id=1, source_target_pairs={{0,1},{1,0},{2,3},{3,2},{4,5},{5,4},{6,7},{7,6},{8,9},{9,8},{10,11... | collective-permute-start | bytes 3932168 | tf_op jit(solution)/shard_map/ppermute | solution.py:192
  34.1 4.6 %collective-permute-start.1 = (f32[5,128]{1,0:T(8,128)S(1)}, f32[5,128]{1,0:T(8,128)}, u32[]{:S(2)}, u32[]{:S(2)}) collective-permute-start(f32[5,128]{1,0:T(8,128)S(1)} %get-tuple-element.13), channel_id=1, source_target_pairs={{0,2},{1,3},{2,0},{3,1},{4,6},{5,7},{6,4},{7,5},{8,10},{9,11},{10,... | collective-permute-start | bytes 7688 | tf_op jit(solution)/shard_map/ppermute | solution.py:192
  35.9 6.1 %collective-permute-start = (f32[5,128]{1,0:T(8,128)S(1)}, f32[5,128]{1,0:T(8,128)}, u32[]{:S(2)}, u32[]{:S(2)}) collective-permute-start(f32[5,128]{1,0:T(8,128)S(1)} %get-tuple-element.13), channel_id=1, source_target_pairs={{0,1},{1,0},{2,3},{3,2},{4,5},{5,4},{6,7},{7,6},{8,9},{9,8},{10,11... | collective-permute-start | bytes 7688 | tf_op jit(solution)/shard_map/ppermute | solution.py:192
  36.1 5.9 %collective-permute-start.7 = (bf16[512,128]{1,0:T(8,128)(2,1)}, bf16[512,128]{1,0:T(8,128)(2,1)S(1)}, u32[]{:S(2)}, u32[]{:S(2)}) collective-permute-start(bf16[512,128]{1,0:T(8,128)(2,1)} %bitcast.27), channel_id=1, source_target_pairs={{0,2},{1,3},{2,0},{3,1},{4,6},{5,7},{6,4},{7,5},{8,10},{9,11},{10,... | collective-permute-start | bytes 393224 | tf_op jit(solution)/shard_map/ppermute | solution.py:192
  36.4 18.6 %copy-start.1 = (bf16[1,4,10,128,128]{4,3,2,1,0:T(8,128)(2,1)S(1)}, bf16[1,4,10,128,128]{4,3,2,1,0:T(8,128)(2,1)}, u32[]{:S(2)}) copy-start(bf16[1,4,10,128,128]{4,3,2,1,0:T(8,128)(2,1)} %param.9) | copy-start | bytes 3932164
  38.7 6.3 %collective-permute-start.6 = (bf16[512,128]{1,0:T(8,128)(2,1)S(1)}, bf16[512,128]{1,0:T(8,128)(2,1)S(1)}, u32[]{:S(2)}, u32[]{:S(2)}) collective-permute-start(bf16[512,128]{1,0:T(8,128)(2,1)S(1)} %bitcast.28), channel_id=1, source_target_pairs={{0,1},{1,0},{2,3},{3,2},{4,5},{5,4},{6,7},{7,6},{8,9},{9,8},{10,11... | collective-permute-start | bytes 393224 | tf_op jit(solution)/shard_map/ppermute | solution.py:192
  42.0 3.5 %collective-permute-start.8 = (bf16[512,128]{1,0:T(8,128)(2,1)S(1)}, bf16[512,128]{1,0:T(8,128)(2,1)}, u32[]{:S(2)}, u32[]{:S(2)}) collective-permute-start(bf16[512,128]{1,0:T(8,128)(2,1)S(1)} %collective-permute-done.7.y2), channel_id=1, source_target_pairs={{0,1},{1,0},{2,3},{3,2},{4,5},{5,4},{6,7},{7,6},{8,9},{9,8},{10,11... | collective-permute-start | bytes 393224 | tf_op jit(solution)/shard_map/ppermute | solution.py:192
  42.0 3.0 %collective-permute-start.2 = (f32[5,128]{1,0:T(8,128)}, f32[5,128]{1,0:T(8,128)}, u32[]{:S(2)}, u32[]{:S(2)}) collective-permute-start(f32[5,128]{1,0:T(8,128)} %collective-permute-done.1), channel_id=1, source_target_pairs={{0,1},{1,0},{2,3},{3,2},{4,5},{5,4},{6,7},{7,6},{8,9},{9,8},{10,11... | collective-permute-start | bytes 7688 | tf_op jit(solution)/shard_map/ppermute | solution.py:192
  45.0 72.9 %collective-permute-start.9 = (bf16[4,128,512]{2,1,0:T(8,128)(2,1)}, bf16[4,128,512]{2,1,0:T(8,128)(2,1)}, u32[]{:S(2)}, u32[]{:S(2)}) collective-permute-start(bf16[4,128,512]{2,1,0:T(8,128)(2,1)} %get-tuple-element.10), channel_id=1, source_target_pairs={{0,1},{1,0},{2,3},{3,2},{4,5},{5,4},{6,7},{7,6},{8,9},{9,8},{10,11... | collective-permute-start | bytes 1572872 | tf_op jit(solution)/shard_map/ppermute | solution.py:192
  45.1 72.9 %collective-permute-start.11 = (bf16[4,128,512]{2,1,0:T(8,128)(2,1)}, bf16[4,128,512]{2,1,0:T(8,128)(2,1)}, u32[]{:S(2)}, u32[]{:S(2)}) collective-permute-start(bf16[4,128,512]{2,1,0:T(8,128)(2,1)} %get-tuple-element.10), channel_id=1, source_target_pairs={{0,3},{1,2},{2,1},{3,0},{4,7},{5,6},{6,5},{7,4},{8,11},{9,10},{10,... | collective-permute-start | bytes 1572872 | tf_op jit(solution)/shard_map/ppermute | solution.py:192
  45.4 72.5 %collective-permute-start.10 = (bf16[4,128,512]{2,1,0:T(8,128)(2,1)S(1)}, bf16[4,128,512]{2,1,0:T(8,128)(2,1)}, u32[]{:S(2)}, u32[]{:S(2)}) collective-permute-start(bf16[4,128,512]{2,1,0:T(8,128)(2,1)S(1)} %get-tuple-element.11.c0), channel_id=1, source_target_pairs={{0,2},{1,3},{2,0},{3,1},{4,6},{5,7},{6,4},{7,5},{8,10},{9,11},{10,... | collective-permute-start | bytes 1572872 | tf_op jit(solution)/shard_map/ppermute | solution.py:192
  55.0 0.7 copy-start.3
  55.7 62.2 %copy-start.5 = (s32[4]{0:T(128)S(1)}, s32[4]{0:T(128)}, u32[]{:S(2)}) copy-start(s32[4]{0:T(128)} %broadcast_xor_fusion.targets) | copy-start | bytes 52
  118.0 0.7 copy-start.4
  121.4 1.3 collective-permute-start.12
  122.8 5.2 %collective-permute-start.13 = (bf16[4,32,128]{2,1,0:T(8,128)(2,1)S(1)}, bf16[4,32,128]{2,1,0:T(8,128)(2,1)S(1)}, u32[]{:S(2)}, u32[]{:S(2)}) collective-permute-start(bf16[4,32,128]{2,1,0:T(8,128)(2,1)S(1)} %slice.56), channel_id=1, source_target_pairs={{0,16},{4,20},{8,24},{12,28},{16,0},{20,4},{24,8},{28,12},{1,17},{... | collective-permute-start | bytes 98312 | tf_op jit(solution)/shard_map/ppermute | solution.py:192
  128.0 3.8 %collective-permute-start.14 = (bf16[2,32,128]{2,1,0:T(8,128)(2,1)S(1)}, bf16[2,32,128]{2,1,0:T(8,128)(2,1)S(1)}, u32[]{:S(2)}, u32[]{:S(2)}) collective-permute-start(bf16[2,32,128]{2,1,0:T(8,128)(2,1)S(1)} %slice.57), channel_id=1, source_target_pairs={{0,8},{4,12},{8,0},{12,4},{16,24},{20,28},{24,16},{28,20},{1,9},{5... | collective-permute-start | bytes 49160 | tf_op jit(solution)/shard_map/ppermute | solution.py:192
  131.9 3.7 %collective-permute-start.15 = (bf16[1,32,128]{2,1,0:T(8,128)(2,1)S(1)}, bf16[1,32,128]{2,1,0:T(8,128)(2,1)S(1)}, u32[]{:S(2)}, u32[]{:S(2)}) collective-permute-start(bf16[1,32,128]{2,1,0:T(8,128)(2,1)S(1)} %slice.58), channel_id=1, source_target_pairs={{0,4},{4,0},{8,12},{12,8},{16,20},{20,16},{24,28},{28,24},{1,5},{5... | collective-permute-start | bytes 24584 | tf_op jit(solution)/shard_map/ppermute | solution.py:192

commit v2 on v1

v2 whole, which is shorter than its diff:
```python
import functools

import jax
import jax.numpy as jnp
from jax import lax
from jax.experimental import pallas as pl
from jax.experimental.pallas import tpu as pltpu
from jax.sharding import PartitionSpec as P

DEG = 4
ITERS = 2
F32 = jnp.float32
BF16 = jnp.bfloat16
GATE_VMEM = 24 << 20
FILTER_VMEM = 24 << 20


def split2(x):
    hi = x.astype(BF16)
    return hi, (x - hi.astype(F32)).astype(BF16)


def inverse_factor(gram):
    n = gram.shape[0]
    lane = lax.broadcasted_iota(jnp.int32, (8, n), 1)
    sub = lax.broadcasted_iota(jnp.int32, (8, n), 0)
    groups = n // 8
    w = [gram[8 * g : 8 * g + 8, :] for g in range(groups)]

    def spread(x):
        return jnp.broadcast_to(x, (8, n))

    for b in range(groups):
        j0 = 8 * b
        inside = (lane >= j0) & (lane < j0 + 8)
        cols = [{g: spread(w[g][:, j0 + c : j0 + c + 1]) for g in range(b, groups)} for c in range(8)]
        z = jnp.where(inside, jnp.where(lane == sub + j0, 1.0, 0.0), w[b])
        for g in range(b + 1, groups):
            w[g] = jnp.where(inside, 0.0, w[g])
        pivots = jnp.ones((8, n), F32)
        for c in range(8):
            pivot = spread(cols[c][b][c : c + 1, :])
            inv = 1.0 / pivot
            pivots = jnp.where(sub == c, pivot, pivots)
            mult = {g: cols[c][g] * inv for g in range(b + 1, groups)}
            if c < 7:
                mult[b] = jnp.where(sub > c, cols[c][b] * inv, 0.0)
            for c2 in range(c + 1, 8):
                entry = spread(cols[c2][b][c : c + 1, :])
                for g in mult:
                    cols[c2][g] = cols[c2][g] - mult[g] * entry
            row = spread(z[c : c + 1, :])
            if c < 7:
                z = z - mult[b] * row
            for g in range(b + 1, groups):
                w[g] = w[g] - mult[g] * row
        w[b] = jnp.where(lane < j0 + 8, z, 0.0) * lax.rsqrt(pivots)
    return jnp.concatenate(w, axis=0).T


def pack_kernel(modes, mass, pattern, out, sem):
    own, nzb = pattern.shape
    width = out.shape[1]
    held = modes.shape[0]
    first = pltpu.make_async_copy(modes, out.at[pl.ds(0, held)], sem.at[0])
    first.start()
    left = jnp.concatenate([mass[:, i * width : (i + 1) * width] for i in range(own)], axis=0)
    pieces = []
    for _ in range(3):
        pieces.append(left.astype(BF16).astype(F32))
        left = left - pieces[-1]
    pieces.append(jnp.concatenate([pattern[...].astype(F32), jnp.zeros((own, width - nzb), F32)], axis=1))
    used = 4 * own
    lines = out.shape[0] - held
    if lines > used:
        pieces.append(jnp.zeros((lines - used, width), F32))
    out[held:, :] = jnp.concatenate(pieces, axis=0).astype(BF16)
    first.wait()


def gate_kernel(*refs):
    del refs


def filter_kernel(
    nranks, own, nzb, low, high, k0, k1, k2, k3, a0, a1, a2, a3, phi_out, theta_out, rs_out,
    stiff, ya, yb, scale, small, codes, pat, ksem, ysem, ssem, psem,
):
    bs = stiff.shape[1]
    nb = own * nranks
    blk = nzb * bs
    held = own * bs
    lines = small.shape[0] // nranks
    me = lax.axis_index("split")
    cut = own * blk
    copies = []
    for t, ref in enumerate((a0, a1, a2, a3)):
        rank = me ^ t
        copies.append(
            pltpu.make_async_copy(
                ref.at[pl.ds(held, lines)],
                small.at[pl.ds(pl.multiple_of(rank * lines, lines), lines)],
                ssem.at[t],
            )
        )
        copies.append(
            pltpu.make_async_copy(
                ref.at[pl.ds(0, held)],
                ya.at[pl.ds(pl.multiple_of(rank * held, held), held)],
                ysem.at[t],
            )
        )
    parts, kcopies = [], []
    for t, ref in enumerate((k0, k1, k2, k3)):
        parts.append((me ^ t) * own)
        dst = stiff.at[pl.ds(pl.multiple_of(parts[-1] * blk, blk), cut)]
        kcopies.append(pltpu.make_async_copy(ref, dst, ksem.at[t]))
    for c in copies + kcopies:
        c.start()
    for c in copies[::2]:
        c.wait()
    mass = []
    for r in range(nranks):
        rows = small[r * lines : (r + 1) * lines, :].astype(F32)
        codes[r * own : (r + 1) * own, :] = rows[3 * own : 4 * own, :].astype(jnp.int32)
        whole = rows[:own] + rows[own : 2 * own] + rows[2 * own : 3 * own]
        mass += [whole[i : i + 1, :] for i in range(own)]
    down = pltpu.make_async_copy(codes, pat, psem.at[0])
    down.start()
    centre = (high[0] + low[0]) / 2.0
    half = (high[0] - low[0]) / 2.0
    for i in range(nb):
        row = jnp.broadcast_to(mass[i], (bs, bs)).T
        scale[i * bs : (i + 1) * bs, :] = 1.0 / (row * half)
    shift = jnp.full((1, 1), centre, F32) / half
    down.wait()
    for c in copies[1::2]:
        c.wait()

    def image(i, src):
        left = jnp.concatenate([stiff[rows_of(i * nzb + k), :] for k in range(nzb)], axis=1)
        right = jnp.concatenate(
            [src[rows_of(pat[i, k]), :] for k in range(nzb)], axis=0
        )
        return jnp.dot(left, right, preferred_element_type=F32)

    def rows_of(i):
        return pl.ds(i * bs if isinstance(i, int) else pl.multiple_of(i * bs, bs), bs)

    def first(i):
        at = rows_of(i)
        yb[at, :] = (image(i, ya) * scale[at, :] - shift * ya[at, :].astype(F32)).astype(BF16)

    def later(i, src, dst):
        at = rows_of(i)
        dst[at, :] = (
            2.0 * (image(i, src) * scale[at, :] - shift * src[at, :].astype(F32)) - dst[at, :].astype(F32)
        ).astype(BF16)

    def sweep(body):
        for i in range(nb):
            body(i)

    def finish():
        src, dst = yb, ya
        for _ in range(DEG - 1):
            sweep(lambda i, src=src, dst=dst: later(i, src, dst))
            src, dst = dst, src
        cur = src
        gram = jnp.zeros((bs, bs), F32)
        for i in range(nb):
            blk = cur[i * bs : (i + 1) * bs, :]
            row = jnp.broadcast_to(mass[i], (bs, bs)).T
            hi, lo = split2(blk.astype(F32) * row)
            both = lax.dot_general(
                blk, jnp.concatenate([hi, lo], axis=1), (((0,), (0,)), ((), ())), preferred_element_type=F32
            )
            gram = gram + both[:, :bs] + both[:, bs:]
        hi, lo = split2(inverse_factor(gram))
        weights = jnp.concatenate([hi, lo], axis=0)
        for i in range(nb):
            blk = cur[i * bs : (i + 1) * bs, :]
            ya[i * bs : (i + 1) * bs, :] = jnp.dot(
                jnp.concatenate([blk, blk], axis=1), weights, preferred_element_type=F32
            ).astype(BF16)

    @pl.loop(0, ITERS)
    def _(it):
        for t, base in enumerate(parts):

            @pl.when(it == 0)
            def _(t=t):
                kcopies[t].wait()

            for r in range(own):
                first(base + r)
        finish()

    theta = jnp.zeros((8, theta_out.shape[1]), F32)
    for i in range(nb):
        at = rows_of(i)
        prod = ya[at, :].astype(F32) * image(i, ya)
        theta = theta + jnp.sum(prod.reshape(-1, 8, prod.shape[1]), axis=0)
    theta = jnp.sum(theta, axis=0, keepdims=True)
    theta_out[...] = theta
    rs_out[...] = jnp.broadcast_to(lax.rsqrt(theta), rs_out.shape)
    phi_out[...] = ya[...]


def product_kernel(phi, rs, c0, c2, out, held, sem):
    me = lax.axis_index("split")
    njs, bs, cols = c0.shape
    copies = []
    for t, ref in enumerate((c0, c2)):
        copies.append(pltpu.make_async_copy(ref, held.at[t], sem.at[t]))
        copies[-1].start()
    prods = None
    for t, c in enumerate(copies):
        c.wait()
        at = pl.multiple_of((me ^ (2 * t)) * cols, cols)
        part = jnp.dot(held[t].reshape(njs * bs, cols), phi[pl.ds(at, cols), :], preferred_element_type=F32)
        prods = part if prods is None else prods + part
    out[...] = (prods * rs[0:1, :]).astype(BF16).reshape(out.shape)


def face_kernel(nranks, nsub, links, slots, mine, other, keep, send, dense):
    me = lax.axis_index("split")
    faces, share, _ = dense.shape
    first = lax.axis_index("sub") * (faces // nsub)
    dense[...] = jnp.zeros_like(dense)
    for j in range(mine.shape[0]):
        hi, lo = split2(mine[j].astype(F32) + other[j].astype(F32))
        left = jnp.concatenate([hi, lo, hi], axis=1)
        right = jnp.concatenate([hi, hi, lo], axis=1)
        rows = left[:share]
        for r in range(1, nranks):
            rows = jnp.where(me == r, left[share * r : share * (r + 1)], rows)
        dense[slots[links[0, j]] ^ first] = lax.dot_general(
            rows, right, (((1,), (1,)), ((), ())), preferred_element_type=F32
        )
    half = faces // 2
    keep[...] = dense[:half]
    send[...] = dense[half:].astype(BF16)


def shards(stiffness, pattern, mass, start_modes, cut_low, cut_high, coupling, incidence, slot_of):
    stiff = stiffness[0]
    own, nzb, bs, _ = stiff.shape
    modes = start_modes.shape[-1]
    nranks = lax.axis_size("split")
    nsub = lax.axis_size("sub")
    nb = own * nranks
    faces = slot_of.shape[0]
    assert nranks == 4 and nsub & (nsub - 1) == 0

    def swap(x, bits, axis="split", n=nranks):
        return lax.ppermute(x, axis, [(i, i ^ bits) for i in range(n)])

    smem = pl.BlockSpec(memory_space=pltpu.SMEM)
    vmem = pl.BlockSpec(memory_space=pltpu.VMEM)
    hbm = pl.BlockSpec(memory_space=pltpu.HBM)
    blocks = stiff.reshape(-1, bs)
    lines = -(-4 * own // 16) * 16
    a_0 = pl.pallas_call(
        pack_kernel,
        out_shape=jax.ShapeDtypeStruct((own * bs + lines, modes), BF16),
        in_specs=[hbm, vmem, vmem],
        out_specs=vmem,
        scratch_shapes=[pltpu.SemaphoreType.DMA((1,))],
        compiler_params=pltpu.CompilerParams(vmem_limit_bytes=GATE_VMEM),
        name="pack",
    )(start_modes[0], mass, pattern[0])
    k_2 = swap(blocks, 2)
    k_1 = swap(blocks, 1)
    a_2 = swap(a_0, 2)
    a_1 = swap(a_0, 1)
    a_3 = swap(a_2, 1)
    k_2 = pl.pallas_call(
        gate_kernel,
        out_shape=jax.ShapeDtypeStruct(k_2.shape, k_2.dtype),
        in_specs=[hbm] * 2,
        out_specs=hbm,
        input_output_aliases={0: 0},
        compiler_params=pltpu.CompilerParams(vmem_limit_bytes=GATE_VMEM),
        name="gate",
    )(k_2, a_2)
    k_3 = swap(k_2, 1)
    c_2 = swap(coupling[0], 2)

    phi, theta, rs = pl.pallas_call(
        functools.partial(filter_kernel, nranks, own, nzb),
        out_shape=(
            jax.ShapeDtypeStruct((nb * bs, modes), BF16),
            jax.ShapeDtypeStruct((1, modes), F32),
            jax.ShapeDtypeStruct((8, modes), F32),
        ),
        in_specs=[smem, smem] + [hbm] * 8,
        out_specs=(vmem, vmem, vmem),
        scratch_shapes=[
            pltpu.VMEM((nb * nzb * bs, bs), BF16),
            pltpu.VMEM((nb * bs, modes), BF16),
            pltpu.VMEM((nb * bs, modes), BF16),
            pltpu.VMEM((nb * bs, modes), F32),
            pltpu.VMEM((nranks * lines, modes), BF16),
            pltpu.VMEM((nb, modes), jnp.int32),
            pltpu.SMEM((nb, modes), jnp.int32),
            pltpu.SemaphoreType.DMA((4,)),
            pltpu.SemaphoreType.DMA((4,)),
            pltpu.SemaphoreType.DMA((4,)),
            pltpu.SemaphoreType.DMA((1,)),
        ],
        compiler_params=pltpu.CompilerParams(vmem_limit_bytes=FILTER_VMEM),
        cost_estimate=pl.CostEstimate(flops=30_000_000_000, bytes_accessed=8 << 20, transcendentals=0),
        name="filter",
    )(cut_low, cut_high, blocks, k_1, k_2, k_3, a_0, a_1, a_2, a_3)

    share = bs // nranks
    nif, _, cols = coupling.shape[1:]
    prods = pl.pallas_call(
        product_kernel,
        out_shape=jax.ShapeDtypeStruct((nif, bs, modes), BF16),
        in_specs=[vmem, vmem, hbm, hbm],
        out_specs=vmem,
        scratch_shapes=[pltpu.VMEM((2, nif, bs, cols), BF16), pltpu.SemaphoreType.DMA((2,))],
        compiler_params=pltpu.CompilerParams(vmem_limit_bytes=16 << 20),
        name="products",
    )(phi, rs, coupling[0], c_2)
    total, send = pl.pallas_call(
        functools.partial(face_kernel, nranks, nsub),
        out_shape=(
            jax.ShapeDtypeStruct((faces // 2, share, bs), F32),
            jax.ShapeDtypeStruct((faces // 2, share, bs), BF16),
        ),
        in_specs=[smem, smem, vmem, vmem],
        out_specs=(vmem, vmem),
        scratch_shapes=[pltpu.VMEM((faces, share, bs), F32)],
        compiler_params=pltpu.CompilerParams(vmem_limit_bytes=16 << 20),
        name="faces",
    )(incidence, slot_of, prods, swap(prods, 1))
    width = nsub // 2
    while True:
        total = total + swap(send, width, "sub", nsub).astype(F32)
        width //= 2
        if not width:
            break
        at = total.shape[0] // 2
        total, send = total[:at], total[at:].astype(BF16)
    return (total, theta)


def solution(mesh):
    placed = (
        P("sub", "split", None, None, None),
        P("sub", "split", None),
        P("sub", "split"),
        P("sub", "split", None),
        P("sub"),
        P("sub"),
        P("sub", None, None, "split"),
        P("sub", None),
        P(),
    )
    return jax.shard_map(
        shards,
        mesh=mesh,
        in_specs=placed,
        out_specs=(P("sub", "split", None), P("sub", None)),
        check_vma=False,
    )
```

time: 137 us -> 84 us (0.61)
  Pallas kernels: 65 us -> 29.7 us
  local copies, waits for them, and re-layouts: 8.74 us -> 2.3 us
  other arithmetic: 6.01 us -> 0.63 us
  waiting for transfers between devices: 40.6 us -> 37.8 us
  starting transfers between devices: 13.7 us -> 11.3 us
    pallas_call x2 -> x5, Pallas kernels: 65 us -> 29.7 us  [the longest x1 27.6 us: shards(): pl.pallas_call(functools.partial(filter_kernel, nranks, own, nzb), out_sh...]
    gather x2 -> x0, local copies, waits for them, and re-layouts: 3 us -> none  [the longest x1 1.86 us: shards(): smalls = jnp.stack([small, s_c, s_x, s_d])[jnp.arange(nranks) ^ me]]
    ppermute x16 -> x11, waiting for transfers between devices: 40.6 us -> 37.8 us  [swap(): return lax.ppermute(x, axis, [(i, i ^ bits) for i in range(n)])]
    ppermute x16 -> x11, starting transfers between devices: 13.7 us -> 11.3 us  [swap(): return lax.ppermute(x, axis, [(i, i ^ bits) for i in range(n)])]
    dynamic_slice x1 -> x0, local copies, waits for them, and re-layouts: 2.2 us -> none  [shards(): other = lax.dynamic_slice_in_dim(coup, (1 - parity) * halfj, halfj, 0)]
    another operation x2 -> x0, other arithmetic: 2.02 us -> none  [shards(): smalls = jnp.stack([small, s_c, s_x, s_d])[jnp.arange(nranks) ^ me]]
    convert_element_type x2 -> x0, other arithmetic: 2.01 us -> none  [the longest x1 1.32 us: shards(): pat_all = smalls[:, -1, :own * nzb].astype(jnp.int32).reshape(nb, nzb)]
  transfers between devices with their start and end apart: 16 -> 11, of which waited for: 6 -> 5; matrix products, arithmetic and copies ran while one was open for 9% -> 0% of each run, Pallas kernels for 46% -> 33%
where the time goes in v2:
time: 84 us; the launch traced here: 83.8 us
  waiting for transfers between devices  37.8 us (45%)
  Pallas kernels  29.7 us (35%)
  starting transfers between devices  11.3 us (13%)
  local copies, waits for them, and re-layouts  2.3 us (3%)
  between operations  2.07 us (2%)
    ppermute x11, waiting for transfers between devices, swap(): return lax.ppermute(x, axis, [(i, i ^ bits) for i in range(n)])  37.8 us
    pallas_call x1, Pallas kernels, shards(): pl.pallas_call(functools.partial(filter_kernel, nranks, own, nzb), out_sh...  27.6 us
    ppermute x11, starting transfers between devices, swap(): return lax.ppermute(x, axis, [(i, i ^ bits) for i in range(n)])  11.3 us
    unnamed x14, local copies, waits for them, and re-layouts  2.29 us
  transfers between devices with their start and end apart: 11, of which 5 were waited for; matrix products, arithmetic and copies ran while one was open for 0% of the time, Pallas kernels for 33%

profile of v2, /device:TPU:0, one launch (start us, length us, event | category | flops | bytes accessed | tf_op | source)
XLA Modules:
  0.0 83.8 jit_solution(16007153984675927483)
XLA Ops:
  0.6 3.0 %collective-permute-start.1 = (bf16[5120,128]{1,0:T(8,128)(2,1)}, bf16[5120,128]{1,0:T(8,128)(2,1)S(1)}, u32[]{:S(2)}, u32[]{:S(2)}) collective-permute-start(bf16[5120,128]{1,0:T(8,128)(2,1)} %bitcast.8), channel_id=1, source_target_pairs={{0,2},{1,3},{2,0},{3,1},{4,6},{5,7},{6,4},{7,5},{8,10},{9,11},{10,... | collective-permute-start | bytes 3932168 | tf_op jit(solution)/shard_map/ppermute | solution.py:257
  3.6 0.0 copy-start.1
  3.6 0.9 %copy-done.1 = bf16[1,512,128]{2,1,0:T(8,128)(2,1)S(1)} copy-done((bf16[1,512,128]{2,1,0:T(8,128)(2,1)S(1)}, bf16[1,512,128]{2,1,0:T(8,128)(2,1)}, u32[]{:S(2)}) %copy-start.1) | copy-done | bytes 131096
  4.5 0.0 copy-start.2
  4.5 0.7 copy-done.2
  5.2 0.0 copy-start.3
  5.2 0.7 copy-done.3
  5.9 0.2 pack.1.a0
  6.1 0.0 copy-start
  6.1 0.0 copy-start.6
  6.1 0.1 collective-permute-start.2
  6.2 0.1 collective-permute-start
  6.2 29.3 %collective-permute-done.2.refs_1_.a2 = bf16[528,128]{1,0:T(8,128)(2,1)S(1)} collective-permute-done((bf16[528,128]{1,0:T(8,128)(2,1)S(1)}, bf16[528,128]{1,0:T(8,128)(2,1)S(1)}, u32[]{:S(2)}, u32[]{:S(2)}) %collective-permute-start.2) | collective-permute-done | bytes 135200 | tf_op jit(solution)/shard_map/ppermute | solution.py:257
  35.5 0.0 collective-permute-done.1.refs_0_
  35.5 0.0 collective-permute-start.3
  35.5 0.5 collective-permute-start.4
  36.0 0.1 collective-permute-start.5
  36.1 0.0 copy-done
  36.1 1.7 %collective-permute-start.6 = (bf16[8,128,512]{2,1,0:T(8,128)(2,1)S(1)}, bf16[8,128,512]{2,1,0:T(8,128)(2,1)S(1)}, u32[]{:S(2)}, u32[]{:S(2)}) collective-permute-start(bf16[8,128,512]{2,1,0:T(8,128)(2,1)S(1)} %bitcast.4), channel_id=1, source_target_pairs={{0,2},{1,3},{2,0},{3,1},{4,6},{5,7},{6,4},{7,5},{8,10},{9,11},{10,... | collective-permute-start | bytes 3145736 | tf_op jit(solution)/shard_map/ppermute | solution.py:257
  39.1 0.0 collective-permute-done.4.a1
  39.1 0.0 collective-permute-done.5.a3
  39.2 0.0 collective-permute-done.k1
  39.2 0.0 collective-permute-done.3.k3
  39.2 0.0 copy-done.6
  39.2 27.6 %filter.1 = (bf16[2048,128]{1,0:T(8,128)(2,1)S(1)}, f32[1,128]{1,0:T(1,128)}, f32[8,128]{1,0:T(8,128)S(1)}) custom-call(f32[1]{0:T(128)S(6)} %copy.13.low, f32[1]{0:T(128)S(6)} %copy.14.high, bf16[5120,128]{1,0:T(8,128)(2,1)S(1)} %bitcast.10, bf16[5120,128]{1,0:T(8,128)(2,1)S(1)} %collective-permute-done.k1, bf16[5120,128]{1,0:T(8,128)(2,1)S(1)} %gate.1.k2, ...), custom_call_target="tpu_custom_call" | custom-call | flops 30000001024 | bytes 8388608 | tf_op jit(solution)/shard_map/filter/pallas_call | solution.py:290
  66.8 0.0 collective-permute-done.6.c2
  66.8 0.0 copy-start.4
  66.8 0.0 copy-start.5
  66.8 1.0 %products.1.mine = bf16[8,128,128]{2,1,0:T(8,128)(2,1)S(1)} custom-call(bf16[2048,128]{1,0:T(8,128)(2,1)S(1)} %get-tuple-element.7.phi, f32[8,128]{1,0:T(8,128)S(1)} %get-tuple-element.8.rs, bf16[8,128,512]{2,1,0:T(8,128)(2,1)S(1)} %bitcast.5, bf16[8,128,512]{2,1,0:T(8,128)(2,1)S(1)} %collective-permute-done.6.c2), custom_call_target="tpu_custom_call" | custom-call | tf_op jit(solution)/shard_map/products/pallas_call | solution.py:319
  67.8 0.2 collective-permute-start.7
  68.0 1.4 %collective-permute-done.7.other = bf16[8,128,128]{2,1,0:T(8,128)(2,1)S(1)} collective-permute-done((bf16[8,128,128]{2,1,0:T(8,128)(2,1)S(1)}, bf16[8,128,128]{2,1,0:T(8,128)(2,1)S(1)}, u32[]{:S(2)}, u32[]{:S(2)}) %collective-permute-start.7) | collective-permute-done | bytes 262176 | tf_op jit(solution)/shard_map/ppermute | solution.py:257
  69.4 0.0 copy-done.4
  69.4 0.0 copy-done.5
  69.4 0.9 %faces.1 = (f32[4,32,128]{2,1,0:T(8,128)S(1)}, bf16[4,32,128]{2,1,0:T(8,128)(2,1)S(1)}) custom-call(s32[1,8]{1,0:T(1,128)S(1)} %copy-done.4, s32[8]{0:T(128)S(1)} %copy-done.5, bf16[8,128,128]{2,1,0:T(8,128)(2,1)S(1)} %products.1.mine, bf16[8,128,128]{2,1,0:T(8,128)(2,1)S(1)} %collective-permute-done.7.other), custom_call_target="tpu_custom_call" | custom-call | tf_op jit(solution)/shard_map/faces/pallas_call | solution.py:328
  70.4 2.7 %collective-permute-start.8 = (bf16[4,32,128]{2,1,0:T(8,128)(2,1)S(1)}, bf16[4,32,128]{2,1,0:T(8,128)(2,1)S(1)}, u32[]{:S(2)}, u32[]{:S(2)}) collective-permute-start(bf16[4,32,128]{2,1,0:T(8,128)(2,1)S(1)} %get-tuple-element.10), channel_id=1, source_target_pairs={{0,16},{4,20},{8,24},{12,28},{16,0},{20,4},{24,8},{28,12},{1,17},{... | collective-permute-start | bytes 98312 | tf_op jit(solution)/shard_map/ppermute | solution.py:257
  73.0 2.6 %collective-permute-done.8 = bf16[4,32,128]{2,1,0:T(8,128)(2,1)S(1)} collective-permute-done((bf16[4,32,128]{2,1,0:T(8,128)(2,1)S(1)}, bf16[4,32,128]{2,1,0:T(8,128)(2,1)S(1)}, u32[]{:S(2)}, u32[]{:S(2)}) %collective-permute-start.8) | collective-permute-done | bytes 32800 | tf_op jit(solution)/shard_map/ppermute | solution.py:257
  75.6 1.3 %collective-permute-start.9 = (bf16[2,32,128]{2,1,0:T(8,128)(2,1)S(1)}, bf16[2,32,128]{2,1,0:T(8,128)(2,1)S(1)}, u32[]{:S(2)}, u32[]{:S(2)}) collective-permute-start(bf16[2,32,128]{2,1,0:T(8,128)(2,1)S(1)} %slice.26), channel_id=1, source_target_pairs={{0,8},{4,12},{8,0},{12,4},{16,24},{20,28},{24,16},{28,20},{1,9},{5... | collective-permute-start | bytes 49160 | tf_op jit(solution)/shard_map/ppermute | solution.py:257
  76.9 2.5 %collective-permute-done.9 = bf16[2,32,128]{2,1,0:T(8,128)(2,1)S(1)} collective-permute-done((bf16[2,32,128]{2,1,0:T(8,128)(2,1)S(1)}, bf16[2,32,128]{2,1,0:T(8,128)(2,1)S(1)}, u32[]{:S(2)}, u32[]{:S(2)}) %collective-permute-start.9) | collective-permute-done | bytes 16416 | tf_op jit(solution)/shard_map/ppermute | solution.py:257
  79.4 1.6 %collective-permute-start.10 = (bf16[1,32,128]{2,1,0:T(8,128)(2,1)S(1)}, bf16[1,32,128]{2,1,0:T(8,128)(2,1)S(1)}, u32[]{:S(2)}, u32[]{:S(2)}) collective-permute-start(bf16[1,32,128]{2,1,0:T(8,128)(2,1)S(1)} %slice.27), channel_id=1, source_target_pairs={{0,4},{4,0},{8,12},{12,8},{16,20},{20,16},{24,28},{28,24},{1,5},{5... | collective-permute-start | bytes 24584 | tf_op jit(solution)/shard_map/ppermute | solution.py:257
  81.0 2.1 %collective-permute-done.10 = bf16[1,32,128]{2,1,0:T(8,128)(2,1)S(1)} collective-permute-done((bf16[1,32,128]{2,1,0:T(8,128)(2,1)S(1)}, bf16[1,32,128]{2,1,0:T(8,128)(2,1)S(1)}, u32[]{:S(2)}, u32[]{:S(2)}) %collective-permute-start.10) | collective-permute-done | bytes 8224 | tf_op jit(solution)/shard_map/ppermute | solution.py:257
  83.2 0.6 slice_add_fusion.1
  (5 shorter events, 0.0 us)
Async XLA Ops:
  0.6 34.9 %collective-permute-start.1 = (bf16[5120,128]{1,0:T(8,128)(2,1)}, bf16[5120,128]{1,0:T(8,128)(2,1)S(1)}, u32[]{:S(2)}, u32[]{:S(2)}) collective-permute-start(bf16[5120,128]{1,0:T(8,128)(2,1)} %bitcast.8), channel_id=1, source_target_pairs={{0,2},{1,3},{2,0},{3,1},{4,6},{5,7},{6,4},{7,5},{8,10},{9,11},{10,... | collective-permute-start | bytes 3932168 | tf_op jit(solution)/shard_map/ppermute | solution.py:257
  3.6 0.9 %copy-start.1 = (bf16[1,512,128]{2,1,0:T(8,128)(2,1)S(1)}, bf16[1,512,128]{2,1,0:T(8,128)(2,1)}, u32[]{:S(2)}) copy-start(bf16[1,512,128]{2,1,0:T(8,128)(2,1)} %param.12) | copy-start | bytes 393220
  4.5 0.7 copy-start.2
  5.2 0.7 copy-start.3
  6.1 30.0 %copy-start = (bf16[1,8,128,512]{3,2,1,0:T(8,128)(2,1)S(1)}, bf16[1,8,128,512]{3,2,1,0:T(8,128)(2,1)}, u32[]{:S(2)}) copy-start(bf16[1,8,128,512]{3,2,1,0:T(8,128)(2,1)} %param.15) | copy-start | bytes 3145732
  6.1 33.1 %copy-start.6 = (bf16[1,4,10,128,128]{4,3,2,1,0:T(8,128)(2,1)S(1)}, bf16[1,4,10,128,128]{4,3,2,1,0:T(8,128)(2,1)}, u32[]{:S(2)}) copy-start(bf16[1,4,10,128,128]{4,3,2,1,0:T(8,128)(2,1)} %param.9) | copy-start | bytes 3932164
  6.1 29.4 %collective-permute-start.2 = (bf16[528,128]{1,0:T(8,128)(2,1)S(1)}, bf16[528,128]{1,0:T(8,128)(2,1)S(1)}, u32[]{:S(2)}, u32[]{:S(2)}) collective-permute-start(bf16[528,128]{1,0:T(8,128)(2,1)S(1)} %pack.1.a0), channel_id=1, source_target_pairs={{0,2},{1,3},{2,0},{3,1},{4,6},{5,7},{6,4},{7,5},{8,10},{9,11},{10,... | collective-permute-start | bytes 405512 | tf_op jit(solution)/shard_map/ppermute | solution.py:257
  6.2 33.0 %collective-permute-start = (bf16[5120,128]{1,0:T(8,128)(2,1)}, bf16[5120,128]{1,0:T(8,128)(2,1)S(1)}, u32[]{:S(2)}, u32[]{:S(2)}) collective-permute-start(bf16[5120,128]{1,0:T(8,128)(2,1)} %bitcast.9), channel_id=1, source_target_pairs={{0,1},{1,0},{2,3},{3,2},{4,5},{5,4},{6,7},{7,6},{8,9},{9,8},{10,11... | collective-permute-start | bytes 3932168 | tf_op jit(solution)/shard_map/ppermute | solution.py:257
  35.5 3.6 %collective-permute-start.3 = (bf16[5120,128]{1,0:T(8,128)(2,1)S(1)}, bf16[5120,128]{1,0:T(8,128)(2,1)S(1)}, u32[]{:S(2)}, u32[]{:S(2)}) collective-permute-start(bf16[5120,128]{1,0:T(8,128)(2,1)S(1)} %gate.1.k2), channel_id=1, source_target_pairs={{0,1},{1,0},{2,3},{3,2},{4,5},{5,4},{6,7},{7,6},{8,9},{9,8},{10,11... | collective-permute-start | bytes 3932168 | tf_op jit(solution)/shard_map/ppermute | solution.py:257
  35.5 3.6 %collective-permute-start.4 = (bf16[528,128]{1,0:T(8,128)(2,1)S(1)}, bf16[528,128]{1,0:T(8,128)(2,1)S(1)}, u32[]{:S(2)}, u32[]{:S(2)}) collective-permute-start(bf16[528,128]{1,0:T(8,128)(2,1)S(1)} %pack.1.a0), channel_id=1, source_target_pairs={{0,1},{1,0},{2,3},{3,2},{4,5},{5,4},{6,7},{7,6},{8,9},{9,8},{10,11... | collective-permute-start | bytes 405512 | tf_op jit(solution)/shard_map/ppermute | solution.py:257
  36.0 3.1 %collective-permute-start.5 = (bf16[528,128]{1,0:T(8,128)(2,1)S(1)}, bf16[528,128]{1,0:T(8,128)(2,1)S(1)}, u32[]{:S(2)}, u32[]{:S(2)}) collective-permute-start(bf16[528,128]{1,0:T(8,128)(2,1)S(1)} %collective-permute-done.2.refs_1_.a2), channel_id=1, source_target_pairs={{0,1},{1,0},{2,3},{3,2},{4,5},{5,4},{6,7},{7,6},{8,9},{9,8},{10,11... | collective-permute-start | bytes 405512 | tf_op jit(solution)/shard_map/ppermute | solution.py:257
  36.1 30.7 %collective-permute-start.6 = (bf16[8,128,512]{2,1,0:T(8,128)(2,1)S(1)}, bf16[8,128,512]{2,1,0:T(8,128)(2,1)S(1)}, u32[]{:S(2)}, u32[]{:S(2)}) collective-permute-start(bf16[8,128,512]{2,1,0:T(8,128)(2,1)S(1)} %bitcast.4), channel_id=1, source_target_pairs={{0,2},{1,3},{2,0},{3,1},{4,6},{5,7},{6,4},{7,5},{8,10},{9,11},{10,... | collective-permute-start | bytes 3145736 | tf_op jit(solution)/shard_map/ppermute | solution.py:257
  66.8 2.6 %copy-start.4 = (s32[1,8]{1,0:T(1,128)S(1)}, s32[1,8]{1,0:T(1,128)}, u32[]{:S(2)}) copy-start(s32[1,8]{1,0:T(1,128)} %links.1) | copy-start | bytes 100
  66.8 2.6 %copy-start.5 = (s32[8]{0:T(128)S(1)}, s32[8]{0:T(128)}, u32[]{:S(2)}) copy-start(s32[8]{0:T(128)} %slots.1) | copy-start | bytes 100
  67.8 1.6 %collective-permute-start.7 = (bf16[8,128,128]{2,1,0:T(8,128)(2,1)S(1)}, bf16[8,128,128]{2,1,0:T(8,128)(2,1)S(1)}, u32[]{:S(2)}, u32[]{:S(2)}) collective-permute-start(bf16[8,128,128]{2,1,0:T(8,128)(2,1)S(1)} %products.1.mine), channel_id=1, source_target_pairs={{0,1},{1,0},{2,3},{3,2},{4,5},{5,4},{6,7},{7,6},{8,9},{9,8},{10,11... | collective-permute-start | bytes 786440 | tf_op jit(solution)/shard_map/ppermute | solution.py:257
  70.4 5.2 %collective-permute-start.8 = (bf16[4,32,128]{2,1,0:T(8,128)(2,1)S(1)}, bf16[4,32,128]{2,1,0:T(8,128)(2,1)S(1)}, u32[]{:S(2)}, u32[]{:S(2)}) collective-permute-start(bf16[4,32,128]{2,1,0:T(8,128)(2,1)S(1)} %get-tuple-element.10), channel_id=1, source_target_pairs={{0,16},{4,20},{8,24},{12,28},{16,0},{20,4},{24,8},{28,12},{1,17},{... | collective-permute-start | bytes 98312 | tf_op jit(solution)/shard_map/ppermute | solution.py:257
  75.6 3.8 %collective-permute-start.9 = (bf16[2,32,128]{2,1,0:T(8,128)(2,1)S(1)}, bf16[2,32,128]{2,1,0:T(8,128)(2,1)S(1)}, u32[]{:S(2)}, u32[]{:S(2)}) collective-permute-start(bf16[2,32,128]{2,1,0:T(8,128)(2,1)S(1)} %slice.26), channel_id=1, source_target_pairs={{0,8},{4,12},{8,0},{12,4},{16,24},{20,28},{24,16},{28,20},{1,9},{5... | collective-permute-start | bytes 49160 | tf_op jit(solution)/shard_map/ppermute | solution.py:257
  79.4 3.7 %collective-permute-start.10 = (bf16[1,32,128]{2,1,0:T(8,128)(2,1)S(1)}, bf16[1,32,128]{2,1,0:T(8,128)(2,1)S(1)}, u32[]{:S(2)}, u32[]{:S(2)}) collective-permute-start(bf16[1,32,128]{2,1,0:T(8,128)(2,1)S(1)} %slice.27), channel_id=1, source_target_pairs={{0,4},{4,0},{8,12},{12,8},{16,20},{20,16},{24,28},{28,24},{1,5},{5... | collective-permute-start | bytes 24584 | tf_op jit(solution)/shard_map/ppermute | solution.py:257

commit v3 on v2

--- a/solution.py
+++ b/solution.py
@@ -20,7 +20,17 @@
     return hi, (x - hi.astype(F32)).astype(BF16)
 
 
-def inverse_factor(gram):
+def split3(x):
+    hi = x.astype(BF16)
+    mid, lo = split2(x - hi.astype(F32))
+    return hi, mid, lo
+
+
+def stack(parts):
+    return jnp.concatenate([p.astype(F32) for p in parts], axis=0).astype(BF16)
+
+
+def inverse_factor(gram, between, near=3):
     n = gram.shape[0]
     lane = lax.broadcasted_iota(jnp.int32, (8, n), 1)
     sub = lax.broadcasted_iota(jnp.int32, (8, n), 0)
@@ -30,31 +40,55 @@
     def spread(x):
         return jnp.broadcast_to(x, (8, n))
 
+    ahead = [spread(w[0][:, c : c + 1]) for c in range(8)]
     for b in range(groups):
         j0 = 8 * b
+        top = min(groups, b + near + 1)
         inside = (lane >= j0) & (lane < j0 + 8)
-        cols = [{g: spread(w[g][:, j0 + c : j0 + c + 1]) for g in range(b, groups)} for c in range(8)]
+        cols = [{b: ahead[c]} for c in range(8)]
+        for g in range(b + 1, top):
+            for c in range(8):
+                cols[c][g] = spread(w[g][:, j0 + c : j0 + c + 1])
+        ahead = []
+        if b + 1 < groups:
+            ahead = [spread(w[b + 1][:, j0 + 8 + c : j0 + 9 + c]) for c in range(8)]
         z = jnp.where(inside, jnp.where(lane == sub + j0, 1.0, 0.0), w[b])
         for g in range(b + 1, groups):
             w[g] = jnp.where(inside, 0.0, w[g])
         pivots = jnp.ones((8, n), F32)
+        inverses = jnp.ones((8, n), F32)
         for c in range(8):
             pivot = spread(cols[c][b][c : c + 1, :])
             inv = 1.0 / pivot
             pivots = jnp.where(sub == c, pivot, pivots)
-            mult = {g: cols[c][g] * inv for g in range(b + 1, groups)}
+            inverses = jnp.where(sub == c, inv, inverses)
+            mult = {g: cols[c][g] * inv for g in range(b + 1, top)}
             if c < 7:
                 mult[b] = jnp.where(sub > c, cols[c][b] * inv, 0.0)
             for c2 in range(c + 1, 8):
                 entry = spread(cols[c2][b][c : c + 1, :])
                 for g in mult:
                     cols[c2][g] = cols[c2][g] - mult[g] * entry
+            for c2 in range(len(ahead)):
+                ahead[c2] = ahead[c2] - mult[b + 1] * spread(cols[c][b + 1][c2 : c2 + 1, :])
             row = spread(z[c : c + 1, :])
             if c < 7:
                 z = z - mult[b] * row
-            for g in range(b + 1, groups):
+            for g in range(b + 1, top):
                 w[g] = w[g] - mult[g] * row
+        if top < groups:
+            a1, a2, a3 = split3(z * inverses)
+            b1, b2, b3 = split3(z)
+            update = lax.dot_general(
+                stack((a1, a1, a2, a2, a1, a3)),
+                stack((b1, b2, b1, b2, b3, b1)),
+                (((0,), (0,)), ((), ())),
+                preferred_element_type=F32,
+            )
+            for g in range(top, groups):
+                w[g] = w[g] - update[8 * g : 8 * g + 8, :]
         w[b] = jnp.where(lane < j0 + 8, z, 0.0) * lax.rsqrt(pivots)
+        between(b)
     return jnp.concatenate(w, axis=0).T
 
 
@@ -84,49 +118,33 @@
 
 def filter_kernel(
     nranks, own, nzb, low, high, k0, k1, k2, k3, a0, a1, a2, a3, phi_out, theta_out, rs_out,
-    stiff, ya, yb, scale, small, codes, pat, ksem, ysem, ssem, psem,
+    ya, yb, zs, scale, codes, pat, psem,
 ):
-    bs = stiff.shape[1]
+    bs = k0.shape[1]
     nb = own * nranks
-    blk = nzb * bs
     held = own * bs
-    lines = small.shape[0] // nranks
     me = lax.axis_index("split")
-    cut = own * blk
-    copies = []
-    for t, ref in enumerate((a0, a1, a2, a3)):
-        rank = me ^ t
-        copies.append(
-            pltpu.make_async_copy(
-                ref.at[pl.ds(held, lines)],
-                small.at[pl.ds(pl.multiple_of(rank * lines, lines), lines)],
-                ssem.at[t],
-            )
-        )
-        copies.append(
-            pltpu.make_async_copy(
-                ref.at[pl.ds(0, held)],
-                ya.at[pl.ds(pl.multiple_of(rank * held, held), held)],
-                ysem.at[t],
-            )
-        )
-    parts, kcopies = [], []
-    for t, ref in enumerate((k0, k1, k2, k3)):
-        parts.append((me ^ t) * own)
-        dst = stiff.at[pl.ds(pl.multiple_of(parts[-1] * blk, blk), cut)]
-        kcopies.append(pltpu.make_async_copy(ref, dst, ksem.at[t]))
-    for c in copies + kcopies:
-        c.start()
-    for c in copies[::2]:
-        c.wait()
-    mass = []
+    kept = (k0, k1, k2, k3)
+
+    def rows_of(i):
+        return pl.ds(i * bs if isinstance(i, int) else pl.multiple_of(i * bs, bs), bs)
+
+    mass = [None] * nb
+    lines = a0.shape[0] - held
+    smalls = [ref[held:, :].astype(F32) for ref in (a0, a1, a2, a3)]
     for r in range(nranks):
-        rows = small[r * lines : (r + 1) * lines, :].astype(F32)
+        rows = smalls[0]
+        for t in range(1, nranks):
+            rows = jnp.where((me ^ t) == r, smalls[t], rows)
+        rows = jnp.where(me == r, smalls[0], rows)
         codes[r * own : (r + 1) * own, :] = rows[3 * own : 4 * own, :].astype(jnp.int32)
         whole = rows[:own] + rows[own : 2 * own] + rows[2 * own : 3 * own]
-        mass += [whole[i : i + 1, :] for i in range(own)]
+        for i in range(own):
+            mass[r * own + i] = whole[i : i + 1, :]
     down = pltpu.make_async_copy(codes, pat, psem.at[0])
     down.start()
+    for t, ref in enumerate((a0, a1, a2, a3)):
+        ya[pl.ds(pl.multiple_of((me ^ t) * held, held), held), :] = ref[:held, :]
     centre = (high[0] + low[0]) / 2.0
     half = (high[0] - low[0]) / 2.0
     for i in range(nb):
@@ -134,76 +152,71 @@
         scale[i * bs : (i + 1) * bs, :] = 1.0 / (row * half)
     shift = jnp.full((1, 1), centre, F32) / half
     down.wait()
-    for c in copies[1::2]:
-        c.wait()
-
-    def image(i, src):
-        left = jnp.concatenate([stiff[rows_of(i * nzb + k), :] for k in range(nzb)], axis=1)
-        right = jnp.concatenate(
-            [src[rows_of(pat[i, k]), :] for k in range(nzb)], axis=0
-        )
+
+    def order():
+        for t in range(nranks):
+            for r in range(own):
+                yield t, r, (me ^ t) * own + r
+
+    def image(t, r, i, src):
+        left = jnp.concatenate([kept[t][rows_of(r * nzb + k), :] for k in range(nzb)], axis=1)
+        right = jnp.concatenate([src[rows_of(pat[i, k]), :] for k in range(nzb)], axis=0)
         return jnp.dot(left, right, preferred_element_type=F32)
 
-    def rows_of(i):
-        return pl.ds(i * bs if isinstance(i, int) else pl.multiple_of(i * bs, bs), bs)
-
-    def first(i):
+    for t, r, i in order():
         at = rows_of(i)
-        yb[at, :] = (image(i, ya) * scale[at, :] - shift * ya[at, :].astype(F32)).astype(BF16)
-
-    def later(i, src, dst):
-        at = rows_of(i)
-        dst[at, :] = (
-            2.0 * (image(i, src) * scale[at, :] - shift * src[at, :].astype(F32)) - dst[at, :].astype(F32)
-        ).astype(BF16)
-
-    def sweep(body):
-        for i in range(nb):
-            body(i)
-
-    def finish():
+        yb[at, :] = (image(t, r, i, ya) * scale[at, :] - shift * ya[at, :].astype(F32)).astype(BF16)
+
+    @pl.loop(0, ITERS)
+    def _(it):
         src, dst = yb, ya
         for _ in range(DEG - 1):
-            sweep(lambda i, src=src, dst=dst: later(i, src, dst))
+            for t, r, i in order():
+                at = rows_of(i)
+                dst[at, :] = (
+                    2.0 * (image(t, r, i, src) * scale[at, :] - shift * src[at, :].astype(F32))
+                    - dst[at, :].astype(F32)
+                ).astype(BF16)
             src, dst = dst, src
         cur = src
         gram = jnp.zeros((bs, bs), F32)
         for i in range(nb):
-            blk = cur[i * bs : (i + 1) * bs, :]
+            blk = cur[rows_of(i), :]
             row = jnp.broadcast_to(mass[i], (bs, bs)).T
             hi, lo = split2(blk.astype(F32) * row)
             both = lax.dot_general(
                 blk, jnp.concatenate([hi, lo], axis=1), (((0,), (0,)), ((), ())), preferred_element_type=F32
             )
             gram = gram + both[:, :bs] + both[:, bs:]
-        hi, lo = split2(inverse_factor(gram))
-        weights = jnp.concatenate([hi, lo], axis=0)
+        todo = list(order())
+
+        def between(b):
+            for t, r, i in todo[nb * b // groups : nb * (b + 1) // groups]:
+                hi, lo = split2(image(t, r, i, cur))
+                zs[rows_of(i), :bs] = hi
+                zs[rows_of(i), bs:] = lo
+
+        groups = bs // 8
+        hi, lo = split2(inverse_factor(gram, between))
+        twice = jnp.concatenate([hi, lo], axis=0)
+        thrice = jnp.concatenate([hi, hi, lo], axis=0)
+        theta = jnp.zeros((8, bs), F32)
         for i in range(nb):
-            blk = cur[i * bs : (i + 1) * bs, :]
-            ya[i * bs : (i + 1) * bs, :] = jnp.dot(
-                jnp.concatenate([blk, blk], axis=1), weights, preferred_element_type=F32
-            ).astype(BF16)
-
-    @pl.loop(0, ITERS)
-    def _(it):
-        for t, base in enumerate(parts):
-
-            @pl.when(it == 0)
-            def _(t=t):
-                kcopies[t].wait()
-
-            for r in range(own):
-                first(base + r)
-        finish()
-
-    theta = jnp.zeros((8, theta_out.shape[1]), F32)
-    for i in range(nb):
-        at = rows_of(i)
-        prod = ya[at, :].astype(F32) * image(i, ya)
-        theta = theta + jnp.sum(prod.reshape(-1, 8, prod.shape[1]), axis=0)
-    theta = jnp.sum(theta, axis=0, keepdims=True)
-    theta_out[...] = theta
-    rs_out[...] = jnp.broadcast_to(lax.rsqrt(theta), rs_out.shape)
+            at = rows_of(i)
+            blk = cur[at, :]
+            phi = jnp.dot(jnp.concatenate([blk, blk], axis=1), twice, preferred_element_type=F32).astype(BF16)
+            both = zs[at, :]
+            img = jnp.dot(
+                jnp.concatenate([both, both[:, :bs]], axis=1), thrice, preferred_element_type=F32
+            )
+            ya[at, :] = phi
+            phi = phi.astype(F32)
+            yb[at, :] = (img * scale[at, :] - shift * phi).astype(BF16)
+            theta = theta + jnp.sum((phi * img).reshape(-1, 8, bs), axis=0)
+        theta = jnp.sum(theta, axis=0, keepdims=True)
+        theta_out[...] = theta
+        rs_out[...] = jnp.broadcast_to(lax.rsqrt(theta), rs_out.shape)
+
     phi_out[...] = ya[...]
 
 
@@ -294,19 +307,15 @@
             jax.ShapeDtypeStruct((1, modes), F32),
             jax.ShapeDtypeStruct((8, modes), F32),
         ),
-        in_specs=[smem, smem] + [hbm] * 8,
+        in_specs=[smem, smem] + [vmem] * 8,
         out_specs=(vmem, vmem, vmem),
         scratch_shapes=[
-            pltpu.VMEM((nb * nzb * bs, bs), BF16),
             pltpu.VMEM((nb * bs, modes), BF16),
             pltpu.VMEM((nb * bs, modes), BF16),
+            pltpu.VMEM((nb * bs, 2 * modes), BF16),
             pltpu.VMEM((nb * bs, modes), F32),
-            pltpu.VMEM((nranks * lines, modes), BF16),
             pltpu.VMEM((nb, modes), jnp.int32),
             pltpu.SMEM((nb, modes), jnp.int32),
-            pltpu.SemaphoreType.DMA((4,)),
-            pltpu.SemaphoreType.DMA((4,)),
-            pltpu.SemaphoreType.DMA((4,)),
             pltpu.SemaphoreType.DMA((1,)),
         ],
         compiler_params=pltpu.CompilerParams(vmem_limit_bytes=FILTER_VMEM),

time: 84 us -> 78.5 us (0.935)
  Pallas kernels: 29.7 us -> 24.2 us
  starting transfers between devices: 11.3 us -> 12.5 us
  waiting for transfers between devices: 37.8 us -> 36.6 us
    pallas_call x1, Pallas kernels: 27.6 us -> 22.1 us  [shards(): pl.pallas_call(functools.partial(filter_kernel, nranks, own, nzb), out_sh...]
    ppermute x11, starting transfers between devices: 11.3 us -> 12.5 us  [swap(): return lax.ppermute(x, axis, [(i, i ^ bits) for i in range(n)])]
    ppermute x11, waiting for transfers between devices: 37.8 us -> 36.6 us  [swap(): return lax.ppermute(x, axis, [(i, i ^ bits) for i in range(n)])]
  transfers between devices with their start and end apart: 11 -> 11, of which waited for: 5 -> 6; matrix products, arithmetic and copies ran while one was open for 0% -> 0% of each run, Pallas kernels for 33% -> 28%
where the time goes in v3:
time: 78.5 us; the launch traced here: 78.3 us
  waiting for transfers between devices  36.6 us (47%)
  Pallas kernels  24.2 us (31%)
  starting transfers between devices  12.5 us (16%)
  local copies, waits for them, and re-layouts  2.3 us (3%)
  between operations  2.05 us (3%)
    ppermute x11, waiting for transfers between devices, swap(): return lax.ppermute(x, axis, [(i, i ^ bits) for i in range(n)])  36.6 us
    pallas_call x1, Pallas kernels, shards(): pl.pallas_call(functools.partial(filter_kernel, nranks, own, nzb), out_sh...  22.1 us
    ppermute x11, starting transfers between devices, swap(): return lax.ppermute(x, axis, [(i, i ^ bits) for i in range(n)])  12.5 us
    unnamed x14, local copies, waits for them, and re-layouts  2.29 us
  transfers between devices with their start and end apart: 11, of which 6 were waited for; matrix products, arithmetic and copies ran while one was open for 0% of the time, Pallas kernels for 28%

profile of v3, /device:TPU:0, one launch (start us, length us, event | category | flops | bytes accessed | tf_op | source)
XLA Modules:
  0.0 78.3 jit_solution(3446631566328036818)
XLA Ops:
  0.6 3.0 %collective-permute-start.1 = (bf16[5120,128]{1,0:T(8,128)(2,1)}, bf16[5120,128]{1,0:T(8,128)(2,1)S(1)}, u32[]{:S(2)}, u32[]{:S(2)}) collective-permute-start(bf16[5120,128]{1,0:T(8,128)(2,1)} %bitcast.8), channel_id=1, source_target_pairs={{0,2},{1,3},{2,0},{3,1},{4,6},{5,7},{6,4},{7,5},{8,10},{9,11},{10,... | collective-permute-start | bytes 3932168 | tf_op jit(solution)/shard_map/ppermute | solution.py:270
  3.6 0.0 copy-start.1
  3.6 0.9 %copy-done.1 = bf16[1,512,128]{2,1,0:T(8,128)(2,1)S(1)} copy-done((bf16[1,512,128]{2,1,0:T(8,128)(2,1)S(1)}, bf16[1,512,128]{2,1,0:T(8,128)(2,1)}, u32[]{:S(2)}) %copy-start.1) | copy-done | bytes 131096
  4.5 0.0 copy-start.2
  4.5 0.7 copy-done.2
  5.2 0.0 copy-start.3
  5.2 0.7 copy-done.3
  5.9 0.2 pack.1.a0
  6.1 0.0 copy-start
  6.1 0.0 copy-start.6
  6.1 0.1 collective-permute-start.2
  6.2 0.1 collective-permute-start
  6.2 29.3 %collective-permute-done.2.refs_1_.a2 = bf16[528,128]{1,0:T(8,128)(2,1)S(1)} collective-permute-done((bf16[528,128]{1,0:T(8,128)(2,1)S(1)}, bf16[528,128]{1,0:T(8,128)(2,1)S(1)}, u32[]{:S(2)}, u32[]{:S(2)}) %collective-permute-start.2) | collective-permute-done | bytes 135200 | tf_op jit(solution)/shard_map/ppermute | solution.py:270
  35.5 0.0 collective-permute-done.1.refs_0_
  35.5 0.0 collective-permute-start.3
  35.5 0.5 collective-permute-start.4
  36.0 0.1 collective-permute-start.5
  36.1 0.0 copy-done
  36.1 1.7 %collective-permute-start.6 = (bf16[8,128,512]{2,1,0:T(8,128)(2,1)S(1)}, bf16[8,128,512]{2,1,0:T(8,128)(2,1)S(1)}, u32[]{:S(2)}, u32[]{:S(2)}) collective-permute-start(bf16[8,128,512]{2,1,0:T(8,128)(2,1)S(1)} %bitcast.4), channel_id=1, source_target_pairs={{0,2},{1,3},{2,0},{3,1},{4,6},{5,7},{6,4},{7,5},{8,10},{9,11},{10,... | collective-permute-start | bytes 3145736 | tf_op jit(solution)/shard_map/ppermute | solution.py:270
  39.1 0.0 collective-permute-done.4.a1
  39.1 0.0 collective-permute-done.5.a3
  39.2 0.0 collective-permute-done.k1
  39.2 0.0 collective-permute-done.3.k3
  39.2 0.0 copy-done.6
  39.2 22.1 %filter.1 = (bf16[2048,128]{1,0:T(8,128)(2,1)S(1)}, f32[1,128]{1,0:T(1,128)}, f32[8,128]{1,0:T(8,128)S(1)}) custom-call(f32[1]{0:T(128)S(6)} %copy.13.low, f32[1]{0:T(128)S(6)} %copy.14.high, bf16[5120,128]{1,0:T(8,128)(2,1)S(1)} %bitcast.10, bf16[5120,128]{1,0:T(8,128)(2,1)S(1)} %collective-permute-done.k1, bf16[5120,128]{1,0:T(8,128)(2,1)S(1)} %gate.1.k2, ...), custom_call_target="tpu_custom_call" | custom-call | flops 30000001024 | bytes 8388608 | tf_op jit(solution)/shard_map/filter/pallas_call | solution.py:303
  61.3 0.3 collective-permute-done.6.c2
  61.6 0.0 copy-start.4
  61.6 0.0 copy-start.5
  61.6 1.0 %products.1.mine = bf16[8,128,128]{2,1,0:T(8,128)(2,1)S(1)} custom-call(bf16[2048,128]{1,0:T(8,128)(2,1)S(1)} %get-tuple-element.7.phi, f32[8,128]{1,0:T(8,128)S(1)} %get-tuple-element.8.rs, bf16[8,128,512]{2,1,0:T(8,128)(2,1)S(1)} %bitcast.5, bf16[8,128,512]{2,1,0:T(8,128)(2,1)S(1)} %collective-permute-done.6.c2), custom_call_target="tpu_custom_call" | custom-call | tf_op jit(solution)/shard_map/products/pallas_call | solution.py:328
  62.6 0.1 collective-permute-start.7
  62.7 1.5 %collective-permute-done.7.other = bf16[8,128,128]{2,1,0:T(8,128)(2,1)S(1)} collective-permute-done((bf16[8,128,128]{2,1,0:T(8,128)(2,1)S(1)}, bf16[8,128,128]{2,1,0:T(8,128)(2,1)S(1)}, u32[]{:S(2)}, u32[]{:S(2)}) %collective-permute-start.7) | collective-permute-done | bytes 262176 | tf_op jit(solution)/shard_map/ppermute | solution.py:270
  64.2 0.0 copy-done.4
  64.2 0.0 copy-done.5
  64.2 0.9 %faces.1 = (f32[4,32,128]{2,1,0:T(8,128)S(1)}, bf16[4,32,128]{2,1,0:T(8,128)(2,1)S(1)}) custom-call(s32[1,8]{1,0:T(1,128)S(1)} %copy-done.4, s32[8]{0:T(128)S(1)} %copy-done.5, bf16[8,128,128]{2,1,0:T(8,128)(2,1)S(1)} %products.1.mine, bf16[8,128,128]{2,1,0:T(8,128)(2,1)S(1)} %collective-permute-done.7.other), custom_call_target="tpu_custom_call" | custom-call | tf_op jit(solution)/shard_map/faces/pallas_call | solution.py:337
  65.1 2.9 %collective-permute-start.8 = (bf16[4,32,128]{2,1,0:T(8,128)(2,1)S(1)}, bf16[4,32,128]{2,1,0:T(8,128)(2,1)S(1)}, u32[]{:S(2)}, u32[]{:S(2)}) collective-permute-start(bf16[4,32,128]{2,1,0:T(8,128)(2,1)S(1)} %get-tuple-element.10), channel_id=1, source_target_pairs={{0,16},{4,20},{8,24},{12,28},{16,0},{20,4},{24,8},{28,12},{1,17},{... | collective-permute-start | bytes 98312 | tf_op jit(solution)/shard_map/ppermute | solution.py:270
  68.0 2.0 %collective-permute-done.8 = bf16[4,32,128]{2,1,0:T(8,128)(2,1)S(1)} collective-permute-done((bf16[4,32,128]{2,1,0:T(8,128)(2,1)S(1)}, bf16[4,32,128]{2,1,0:T(8,128)(2,1)S(1)}, u32[]{:S(2)}, u32[]{:S(2)}) %collective-permute-start.8) | collective-permute-done | bytes 32800 | tf_op jit(solution)/shard_map/ppermute | solution.py:270
  70.0 1.9 %collective-permute-start.9 = (bf16[2,32,128]{2,1,0:T(8,128)(2,1)S(1)}, bf16[2,32,128]{2,1,0:T(8,128)(2,1)S(1)}, u32[]{:S(2)}, u32[]{:S(2)}) collective-permute-start(bf16[2,32,128]{2,1,0:T(8,128)(2,1)S(1)} %slice.26), channel_id=1, source_target_pairs={{0,8},{4,12},{8,0},{12,4},{16,24},{20,28},{24,16},{28,20},{1,9},{5... | collective-permute-start | bytes 49160 | tf_op jit(solution)/shard_map/ppermute | solution.py:270
  71.9 1.9 %collective-permute-done.9 = bf16[2,32,128]{2,1,0:T(8,128)(2,1)S(1)} collective-permute-done((bf16[2,32,128]{2,1,0:T(8,128)(2,1)S(1)}, bf16[2,32,128]{2,1,0:T(8,128)(2,1)S(1)}, u32[]{:S(2)}, u32[]{:S(2)}) %collective-permute-start.9) | collective-permute-done | bytes 16416 | tf_op jit(solution)/shard_map/ppermute | solution.py:270
  73.9 2.2 %collective-permute-start.10 = (bf16[1,32,128]{2,1,0:T(8,128)(2,1)S(1)}, bf16[1,32,128]{2,1,0:T(8,128)(2,1)S(1)}, u32[]{:S(2)}, u32[]{:S(2)}) collective-permute-start(bf16[1,32,128]{2,1,0:T(8,128)(2,1)S(1)} %slice.27), channel_id=1, source_target_pairs={{0,4},{4,0},{8,12},{12,8},{16,20},{20,16},{24,28},{28,24},{1,5},{5... | collective-permute-start | bytes 24584 | tf_op jit(solution)/shard_map/ppermute | solution.py:270
  76.0 1.6 %collective-permute-done.10 = bf16[1,32,128]{2,1,0:T(8,128)(2,1)S(1)} collective-permute-done((bf16[1,32,128]{2,1,0:T(8,128)(2,1)S(1)}, bf16[1,32,128]{2,1,0:T(8,128)(2,1)S(1)}, u32[]{:S(2)}, u32[]{:S(2)}) %collective-permute-start.10) | collective-permute-done | bytes 8224 | tf_op jit(solution)/shard_map/ppermute | solution.py:270
  77.7 0.6 slice_add_fusion.1
  (5 shorter events, 0.0 us)
Async XLA Ops:
  0.6 34.9 %collective-permute-start.1 = (bf16[5120,128]{1,0:T(8,128)(2,1)}, bf16[5120,128]{1,0:T(8,128)(2,1)S(1)}, u32[]{:S(2)}, u32[]{:S(2)}) collective-permute-start(bf16[5120,128]{1,0:T(8,128)(2,1)} %bitcast.8), channel_id=1, source_target_pairs={{0,2},{1,3},{2,0},{3,1},{4,6},{5,7},{6,4},{7,5},{8,10},{9,11},{10,... | collective-permute-start | bytes 3932168 | tf_op jit(solution)/shard_map/ppermute | solution.py:270
  3.6 0.9 %copy-start.1 = (bf16[1,512,128]{2,1,0:T(8,128)(2,1)S(1)}, bf16[1,512,128]{2,1,0:T(8,128)(2,1)}, u32[]{:S(2)}) copy-start(bf16[1,512,128]{2,1,0:T(8,128)(2,1)} %param.12) | copy-start | bytes 393220
  4.5 0.7 copy-start.2
  5.2 0.7 copy-start.3
  6.1 30.0 %copy-start = (bf16[1,8,128,512]{3,2,1,0:T(8,128)(2,1)S(1)}, bf16[1,8,128,512]{3,2,1,0:T(8,128)(2,1)}, u32[]{:S(2)}) copy-start(bf16[1,8,128,512]{3,2,1,0:T(8,128)(2,1)} %param.15) | copy-start | bytes 3145732
  6.1 33.1 %copy-start.6 = (bf16[1,4,10,128,128]{4,3,2,1,0:T(8,128)(2,1)S(1)}, bf16[1,4,10,128,128]{4,3,2,1,0:T(8,128)(2,1)}, u32[]{:S(2)}) copy-start(bf16[1,4,10,128,128]{4,3,2,1,0:T(8,128)(2,1)} %param.9) | copy-start | bytes 3932164
  6.1 29.4 %collective-permute-start.2 = (bf16[528,128]{1,0:T(8,128)(2,1)S(1)}, bf16[528,128]{1,0:T(8,128)(2,1)S(1)}, u32[]{:S(2)}, u32[]{:S(2)}) collective-permute-start(bf16[528,128]{1,0:T(8,128)(2,1)S(1)} %pack.1.a0), channel_id=1, source_target_pairs={{0,2},{1,3},{2,0},{3,1},{4,6},{5,7},{6,4},{7,5},{8,10},{9,11},{10,... | collective-permute-start | bytes 405512 | tf_op jit(solution)/shard_map/ppermute | solution.py:270
  6.2 33.0 %collective-permute-start = (bf16[5120,128]{1,0:T(8,128)(2,1)}, bf16[5120,128]{1,0:T(8,128)(2,1)S(1)}, u32[]{:S(2)}, u32[]{:S(2)}) collective-permute-start(bf16[5120,128]{1,0:T(8,128)(2,1)} %bitcast.9), channel_id=1, source_target_pairs={{0,1},{1,0},{2,3},{3,2},{4,5},{5,4},{6,7},{7,6},{8,9},{9,8},{10,11... | collective-permute-start | bytes 3932168 | tf_op jit(solution)/shard_map/ppermute | solution.py:270
  35.5 3.6 %collective-permute-start.3 = (bf16[5120,128]{1,0:T(8,128)(2,1)S(1)}, bf16[5120,128]{1,0:T(8,128)(2,1)S(1)}, u32[]{:S(2)}, u32[]{:S(2)}) collective-permute-start(bf16[5120,128]{1,0:T(8,128)(2,1)S(1)} %gate.1.k2), channel_id=1, source_target_pairs={{0,1},{1,0},{2,3},{3,2},{4,5},{5,4},{6,7},{7,6},{8,9},{9,8},{10,11... | collective-permute-start | bytes 3932168 | tf_op jit(solution)/shard_map/ppermute | solution.py:270
  35.5 3.6 %collective-permute-start.4 = (bf16[528,128]{1,0:T(8,128)(2,1)S(1)}, bf16[528,128]{1,0:T(8,128)(2,1)S(1)}, u32[]{:S(2)}, u32[]{:S(2)}) collective-permute-start(bf16[528,128]{1,0:T(8,128)(2,1)S(1)} %pack.1.a0), channel_id=1, source_target_pairs={{0,1},{1,0},{2,3},{3,2},{4,5},{5,4},{6,7},{7,6},{8,9},{9,8},{10,11... | collective-permute-start | bytes 405512 | tf_op jit(solution)/shard_map/ppermute | solution.py:270
  36.0 3.1 %collective-permute-start.5 = (bf16[528,128]{1,0:T(8,128)(2,1)S(1)}, bf16[528,128]{1,0:T(8,128)(2,1)S(1)}, u32[]{:S(2)}, u32[]{:S(2)}) collective-permute-start(bf16[528,128]{1,0:T(8,128)(2,1)S(1)} %collective-permute-done.2.refs_1_.a2), channel_id=1, source_target_pairs={{0,1},{1,0},{2,3},{3,2},{4,5},{5,4},{6,7},{7,6},{8,9},{9,8},{10,11... | collective-permute-start | bytes 405512 | tf_op jit(solution)/shard_map/ppermute | solution.py:270
  36.1 25.5 %collective-permute-start.6 = (bf16[8,128,512]{2,1,0:T(8,128)(2,1)S(1)}, bf16[8,128,512]{2,1,0:T(8,128)(2,1)S(1)}, u32[]{:S(2)}, u32[]{:S(2)}) collective-permute-start(bf16[8,128,512]{2,1,0:T(8,128)(2,1)S(1)} %bitcast.4), channel_id=1, source_target_pairs={{0,2},{1,3},{2,0},{3,1},{4,6},{5,7},{6,4},{7,5},{8,10},{9,11},{10,... | collective-permute-start | bytes 3145736 | tf_op jit(solution)/shard_map/ppermute | solution.py:270
  61.6 2.6 %copy-start.4 = (s32[1,8]{1,0:T(1,128)S(1)}, s32[1,8]{1,0:T(1,128)}, u32[]{:S(2)}) copy-start(s32[1,8]{1,0:T(1,128)} %links.1) | copy-start | bytes 100
  61.6 2.6 %copy-start.5 = (s32[8]{0:T(128)S(1)}, s32[8]{0:T(128)}, u32[]{:S(2)}) copy-start(s32[8]{0:T(128)} %slots.1) | copy-start | bytes 100
  62.6 1.6 %collective-permute-start.7 = (bf16[8,128,128]{2,1,0:T(8,128)(2,1)S(1)}, bf16[8,128,128]{2,1,0:T(8,128)(2,1)S(1)}, u32[]{:S(2)}, u32[]{:S(2)}) collective-permute-start(bf16[8,128,128]{2,1,0:T(8,128)(2,1)S(1)} %products.1.mine), channel_id=1, source_target_pairs={{0,1},{1,0},{2,3},{3,2},{4,5},{5,4},{6,7},{7,6},{8,9},{9,8},{10,11... | collective-permute-start | bytes 786440 | tf_op jit(solution)/shard_map/ppermute | solution.py:270
  65.1 4.9 %collective-permute-start.8 = (bf16[4,32,128]{2,1,0:T(8,128)(2,1)S(1)}, bf16[4,32,128]{2,1,0:T(8,128)(2,1)S(1)}, u32[]{:S(2)}, u32[]{:S(2)}) collective-permute-start(bf16[4,32,128]{2,1,0:T(8,128)(2,1)S(1)} %get-tuple-element.10), channel_id=1, source_target_pairs={{0,16},{4,20},{8,24},{12,28},{16,0},{20,4},{24,8},{28,12},{1,17},{... | collective-permute-start | bytes 98312 | tf_op jit(solution)/shard_map/ppermute | solution.py:270
  70.0 3.8 %collective-permute-start.9 = (bf16[2,32,128]{2,1,0:T(8,128)(2,1)S(1)}, bf16[2,32,128]{2,1,0:T(8,128)(2,1)S(1)}, u32[]{:S(2)}, u32[]{:S(2)}) collective-permute-start(bf16[2,32,128]{2,1,0:T(8,128)(2,1)S(1)} %slice.26), channel_id=1, source_target_pairs={{0,8},{4,12},{8,0},{12,4},{16,24},{20,28},{24,16},{28,20},{1,9},{5... | collective-permute-start | bytes 49160 | tf_op jit(solution)/shard_map/ppermute | solution.py:270
  73.9 3.8 %collective-permute-start.10 = (bf16[1,32,128]{2,1,0:T(8,128)(2,1)S(1)}, bf16[1,32,128]{2,1,0:T(8,128)(2,1)S(1)}, u32[]{:S(2)}, u32[]{:S(2)}) collective-permute-start(bf16[1,32,128]{2,1,0:T(8,128)(2,1)S(1)} %slice.27), channel_id=1, source_target_pairs={{0,4},{4,0},{8,12},{12,8},{16,20},{20,16},{24,28},{28,24},{1,5},{5... | collective-permute-start | bytes 24584 | tf_op jit(solution)/shard_map/ppermute | solution.py:270

commit v4 on v3

--- a/solution.py
+++ b/solution.py
@@ -11,6 +11,9 @@
 ITERS = 2
 F32 = jnp.float32
 BF16 = jnp.bfloat16
+XFLOPS = 5_000_000_000
+FFLOPS = 1_000_000_000
+SPLIT = 2
 GATE_VMEM = 24 << 20
 FILTER_VMEM = 24 << 20
 
@@ -92,7 +95,8 @@
     return jnp.concatenate(w, axis=0).T
 
 
-def pack_kernel(modes, mass, pattern, out, sem):
+def pack_kernel(modes, mass, pattern, blocks, out, sem):
+    del blocks
     own, nzb = pattern.shape
     width = out.shape[1]
     held = modes.shape[0]
@@ -117,14 +121,20 @@
 
 
 def filter_kernel(
-    nranks, own, nzb, low, high, k0, k1, k2, k3, a0, a1, a2, a3, phi_out, theta_out, rs_out,
-    ya, yb, zs, scale, codes, pat, psem,
+    nranks, own, nzb, low, high, k0, k1, k2, *refs,
 ):
+    k3, refs = refs[:SPLIT], refs[SPLIT:]
+    (
+        a0, a1, a2, a3, phi_out, theta_out, rs_out,
+        ya, yb, zs, scale, heavy, codes, pat, mine, psem, ksem,
+    ) = refs
+    fetch = pltpu.make_async_copy(k0, mine, ksem.at[0])
+    fetch.start()
     bs = k0.shape[1]
     nb = own * nranks
     held = own * bs
     me = lax.axis_index("split")
-    kept = (k0, k1, k2, k3)
+    kept = (mine, k1, k2)
 
     def rows_of(i):
         return pl.ds(i * bs if isinstance(i, int) else pl.multiple_of(i * bs, bs), bs)
@@ -149,6 +159,7 @@
     half = (high[0] - low[0]) / 2.0
     for i in range(nb):
         row = jnp.broadcast_to(mass[i], (bs, bs)).T
+        heavy[i * bs : (i + 1) * bs, :] = row
         scale[i * bs : (i + 1) * bs, :] = 1.0 / (row * half)
     shift = jnp.full((1, 1), centre, F32) / half
     down.wait()
@@ -159,11 +170,18 @@
                 yield t, r, (me ^ t) * own + r
 
     def image(t, r, i, src):
-        left = jnp.concatenate([kept[t][rows_of(r * nzb + k), :] for k in range(nzb)], axis=1)
+        if t < 3:
+            left = [kept[t][rows_of(r * nzb + k), :] for k in range(nzb)]
+        else:
+            per = own // SPLIT
+            left = [k3[r // per][rows_of(r % per * nzb + k), :] for k in range(nzb)]
+        left = jnp.concatenate(left, axis=1)
         right = jnp.concatenate([src[rows_of(pat[i, k]), :] for k in range(nzb)], axis=0)
         return jnp.dot(left, right, preferred_element_type=F32)
 
-    for t, r, i in order():
+    for t, r, i in sorted(order(), key=lambda x: x[0] == 0):
+        if (t, r) == (0, 0):
+            fetch.wait()
         at = rows_of(i)
         yb[at, :] = (image(t, r, i, ya) * scale[at, :] - shift * ya[at, :].astype(F32)).astype(BF16)
 
@@ -182,8 +200,7 @@
         gram = jnp.zeros((bs, bs), F32)
         for i in range(nb):
             blk = cur[rows_of(i), :]
-            row = jnp.broadcast_to(mass[i], (bs, bs)).T
-            hi, lo = split2(blk.astype(F32) * row)
+            hi, lo = split2(blk.astype(F32) * heavy[rows_of(i), :])
             both = lax.dot_general(
                 blk, jnp.concatenate([hi, lo], axis=1), (((0,), (0,)), ((), ())), preferred_element_type=F32
             )
@@ -192,23 +209,18 @@
 
         def between(b):
             for t, r, i in todo[nb * b // groups : nb * (b + 1) // groups]:
-                hi, lo = split2(image(t, r, i, cur))
-                zs[rows_of(i), :bs] = hi
-                zs[rows_of(i), bs:] = lo
+                zs[rows_of(i), :] = image(t, r, i, cur).astype(BF16)
 
         groups = bs // 8
         hi, lo = split2(inverse_factor(gram, between))
         twice = jnp.concatenate([hi, lo], axis=0)
-        thrice = jnp.concatenate([hi, hi, lo], axis=0)
         theta = jnp.zeros((8, bs), F32)
         for i in range(nb):
             at = rows_of(i)
             blk = cur[at, :]
             phi = jnp.dot(jnp.concatenate([blk, blk], axis=1), twice, preferred_element_type=F32).astype(BF16)
-            both = zs[at, :]
-            img = jnp.dot(
-                jnp.concatenate([both, both[:, :bs]], axis=1), thrice, preferred_element_type=F32
-            )
+            blk = zs[at, :]
+            img = jnp.dot(jnp.concatenate([blk, blk], axis=1), twice, preferred_element_type=F32)
             ya[at, :] = phi
             phi = phi.astype(F32)
             yb[at, :] = (img * scale[at, :] - shift * phi).astype(BF16)
@@ -277,27 +289,38 @@
     a_0 = pl.pallas_call(
         pack_kernel,
         out_shape=jax.ShapeDtypeStruct((own * bs + lines, modes), BF16),
-        in_specs=[hbm, vmem, vmem],
+        in_specs=[hbm, vmem, vmem, hbm],
         out_specs=vmem,
         scratch_shapes=[pltpu.SemaphoreType.DMA((1,))],
         compiler_params=pltpu.CompilerParams(vmem_limit_bytes=GATE_VMEM),
         name="pack",
-    )(start_modes[0], mass, pattern[0])
+    )(start_modes[0], mass, pattern[0], blocks)
     k_2 = swap(blocks, 2)
     k_1 = swap(blocks, 1)
     a_2 = swap(a_0, 2)
     a_1 = swap(a_0, 1)
-    a_3 = swap(a_2, 1)
-    k_2 = pl.pallas_call(
+    a_2 = pl.pallas_call(
         gate_kernel,
-        out_shape=jax.ShapeDtypeStruct(k_2.shape, k_2.dtype),
+        out_shape=jax.ShapeDtypeStruct(a_2.shape, a_2.dtype),
         in_specs=[hbm] * 2,
         out_specs=hbm,
         input_output_aliases={0: 0},
         compiler_params=pltpu.CompilerParams(vmem_limit_bytes=GATE_VMEM),
         name="gate",
-    )(k_2, a_2)
-    k_3 = swap(k_2, 1)
+    )(a_2, a_1)
+    a_3 = swap(a_2, 1)
+    a_3 = pl.pallas_call(
+        gate_kernel,
+        out_shape=jax.ShapeDtypeStruct(a_3.shape, a_3.dtype),
+        in_specs=[hbm],
+        out_specs=hbm,
+        input_output_aliases={0: 0},
+        compiler_params=pltpu.CompilerParams(vmem_limit_bytes=GATE_VMEM),
+        cost_estimate=pl.CostEstimate(flops=XFLOPS, bytes_accessed=0, transcendentals=0),
+        name="gate",
+    )(a_3)
+    part = k_2.shape[0] // SPLIT
+    k_3 = [swap(k_2[i * part : (i + 1) * part], 1) for i in range(SPLIT)]
     c_2 = swap(coupling[0], 2)
 
     phi, theta, rs = pl.pallas_call(
@@ -307,21 +330,24 @@
             jax.ShapeDtypeStruct((1, modes), F32),
             jax.ShapeDtypeStruct((8, modes), F32),
         ),
-        in_specs=[smem, smem] + [vmem] * 8,
+        in_specs=[smem, smem, hbm] + [vmem] * (6 + SPLIT),
         out_specs=(vmem, vmem, vmem),
         scratch_shapes=[
             pltpu.VMEM((nb * bs, modes), BF16),
             pltpu.VMEM((nb * bs, modes), BF16),
-            pltpu.VMEM((nb * bs, 2 * modes), BF16),
+            pltpu.VMEM((nb * bs, modes), BF16),
+            pltpu.VMEM((nb * bs, modes), F32),
             pltpu.VMEM((nb * bs, modes), F32),
             pltpu.VMEM((nb, modes), jnp.int32),
             pltpu.SMEM((nb, modes), jnp.int32),
+            pltpu.VMEM(blocks.shape, BF16),
+            pltpu.SemaphoreType.DMA((1,)),
             pltpu.SemaphoreType.DMA((1,)),
         ],
         compiler_params=pltpu.CompilerParams(vmem_limit_bytes=FILTER_VMEM),
-        cost_estimate=pl.CostEstimate(flops=30_000_000_000, bytes_accessed=8 << 20, transcendentals=0),
+        cost_estimate=pl.CostEstimate(flops=FFLOPS, bytes_accessed=8 << 20, transcendentals=0),
         name="filter",
-    )(cut_low, cut_high, blocks, k_1, k_2, k_3, a_0, a_1, a_2, a_3)
+    )(cut_low, cut_high, blocks, k_1, k_2, *k_3, a_0, a_1, a_2, a_3)
 
     share = bs // nranks
     nif, _, cols = coupling.shape[1:]

time: 78.5 us -> 76.2 us (0.971)
  waiting for transfers between devices: 36.6 us -> 34.1 us
  starting transfers between devices: 12.5 us -> 13.5 us
  Pallas kernels: 24.2 us -> 23.3 us
    ppermute x11 -> x12, waiting for transfers between devices: 36.6 us -> 34.1 us  [swap(): return lax.ppermute(x, axis, [(i, i ^ bits) for i in range(n)])]
    ppermute x11 -> x12, starting transfers between devices: 12.5 us -> 13.5 us  [swap(): return lax.ppermute(x, axis, [(i, i ^ bits) for i in range(n)])]
    pallas_call x1, Pallas kernels: 22.1 us -> 21.2 us  [shards(): pl.pallas_call(functools.partial(filter_kernel, nranks, own, nzb), out_sh...]
    unnamed x14 -> x12, local copies, waits for them, and re-layouts: 2.29 us -> 2.28 us
  transfers between devices with their start and end apart: 11 -> 12, of which waited for: 6 -> 7; matrix products, arithmetic and copies ran while one was open for 0% -> 0% of each run, Pallas kernels for 28% -> 28%
where the time goes in v4:
time: 76.2 us; the launch traced here: 76 us
  waiting for transfers between devices  34.1 us (45%)
  Pallas kernels  23.3 us (31%)
  starting transfers between devices  13.5 us (18%)
  local copies, waits for them, and re-layouts  2.38 us (3%)
  between operations  2.05 us (3%)
    ppermute x12, waiting for transfers between devices, swap(): return lax.ppermute(x, axis, [(i, i ^ bits) for i in range(n)])  34.1 us
    pallas_call x1, Pallas kernels, shards(): pl.pallas_call(functools.partial(filter_kernel, nranks, own, nzb), out_sh...  21.2 us
    ppermute x12, starting transfers between devices, swap(): return lax.ppermute(x, axis, [(i, i ^ bits) for i in range(n)])  13.5 us
    unnamed x12, local copies, waits for them, and re-layouts  2.28 us
  transfers between devices with their start and end apart: 12, of which 7 were waited for; matrix products, arithmetic and copies ran while one was open for 0% of the time, Pallas kernels for 28%

profile of v4, /device:TPU:0, one launch (start us, length us, event | category | flops | bytes accessed | tf_op | source)
XLA Modules:
  0.0 76.0 jit_solution(14001459315590540585)
XLA Ops:
  0.6 0.0 copy-start
  0.6 3.0 %collective-permute-start.1 = (bf16[5120,128]{1,0:T(8,128)(2,1)}, bf16[5120,128]{1,0:T(8,128)(2,1)S(1)}, u32[]{:S(2)}, u32[]{:S(2)}) collective-permute-start(bf16[5120,128]{1,0:T(8,128)(2,1)} %bitcast.blocks.k0), channel_id=1, source_target_pairs={{0,2},{1,3},{2,0},{3,1},{4,6},{5,7},{6,4},{7,5},{8,10},{9,11},{10,... | collective-permute-start | bytes 3932168 | tf_op jit(solution)/shard_map/ppermute | solution.py:282
  3.6 0.0 copy-start.1
  3.6 0.9 %copy-done.1 = bf16[1,512,128]{2,1,0:T(8,128)(2,1)S(1)} copy-done((bf16[1,512,128]{2,1,0:T(8,128)(2,1)S(1)}, bf16[1,512,128]{2,1,0:T(8,128)(2,1)}, u32[]{:S(2)}) %copy-start.1) | copy-done | bytes 131096
  4.5 0.0 copy-start.2
  4.6 0.7 copy-done.2
  5.2 0.0 copy-start.3
  5.2 0.7 copy-done.3
  5.9 0.2 pack.1.refs_2_
  6.1 0.1 collective-permute-start.4
  6.2 0.2 collective-permute-start.5
  6.3 0.3 collective-permute-start
  6.7 0.0 copy-done
  6.7 1.8 %collective-permute-start.7 = (bf16[8,128,512]{2,1,0:T(8,128)(2,1)S(1)}, bf16[8,128,512]{2,1,0:T(8,128)(2,1)S(1)}, u32[]{:S(2)}, u32[]{:S(2)}) collective-permute-start(bf16[8,128,512]{2,1,0:T(8,128)(2,1)S(1)} %bitcast.4), channel_id=1, source_target_pairs={{0,2},{1,3},{2,0},{3,1},{4,6},{5,7},{6,4},{7,5},{8,10},{9,11},{10,... | collective-permute-start | bytes 3145736 | tf_op jit(solution)/shard_map/ppermute | solution.py:282
  8.4 25.0 %collective-permute-done.1.k2 = bf16[5120,128]{1,0:T(8,128)(2,1)S(1)} collective-permute-done((bf16[5120,128]{1,0:T(8,128)(2,1)}, bf16[5120,128]{1,0:T(8,128)(2,1)S(1)}, u32[]{:S(2)}, u32[]{:S(2)}) %collective-permute-start.1) | collective-permute-done | bytes 1310752 | tf_op jit(solution)/shard_map/ppermute | solution.py:282
  33.5 0.1 fusion
  33.6 0.1 collective-permute-start.2
  33.6 0.0 collective-permute-done.4.refs_1_.refs_3_
  33.6 0.5 collective-permute-start.3
  34.1 2.2 %collective-permute-done.5.refs_0_ = bf16[528,128]{1,0:T(8,128)(2,1)S(1)} collective-permute-done((bf16[528,128]{1,0:T(8,128)(2,1)S(1)}, bf16[528,128]{1,0:T(8,128)(2,1)S(1)}, u32[]{:S(2)}, u32[]{:S(2)}) %collective-permute-start.5) | collective-permute-done | bytes 135200 | tf_op jit(solution)/shard_map/ppermute | solution.py:282
  36.4 0.0 collective-permute-start.6
  37.7 0.1 collective-permute-done.6.refs_0_
  37.7 0.0 collective-permute-done.k1
  37.7 0.0 collective-permute-done.2.refs_0_
  37.7 0.0 collective-permute-done.3.refs_1_
  37.7 21.2 %filter.1 = (bf16[2048,128]{1,0:T(8,128)(2,1)S(1)}, f32[1,128]{1,0:T(1,128)}, f32[8,128]{1,0:T(8,128)S(1)}) custom-call(f32[1]{0:T(128)S(6)} %copy.15.low, f32[1]{0:T(128)S(6)} %copy.16.high, bf16[5120,128]{1,0:T(8,128)(2,1)} %bitcast.blocks.k0, bf16[5120,128]{1,0:T(8,128)(2,1)S(1)} %collective-permute-done.k1, ...), custom_call_target="tpu_custom_call" | custom-call | flops 1000000000 | bytes 8388608 | tf_op jit(solution)/shard_map/filter/pallas_call | solution.py:326
  59.0 0.0 collective-permute-done.7.c2
  59.0 0.0 copy-start.4
  59.0 0.0 copy-start.5
  59.0 1.0 %products.1.mine = bf16[8,128,128]{2,1,0:T(8,128)(2,1)S(1)} custom-call(bf16[2048,128]{1,0:T(8,128)(2,1)S(1)} %get-tuple-element.7.phi, f32[8,128]{1,0:T(8,128)S(1)} %get-tuple-element.8.rs, bf16[8,128,512]{2,1,0:T(8,128)(2,1)S(1)} %bitcast.5, bf16[8,128,512]{2,1,0:T(8,128)(2,1)S(1)} %collective-permute-done.7.c2), custom_call_target="tpu_custom_call" | custom-call | tf_op jit(solution)/shard_map/products/pallas_call | solution.py:354
  60.0 0.6 collective-permute-start.8
  60.5 1.2 %collective-permute-done.8.other = bf16[8,128,128]{2,1,0:T(8,128)(2,1)S(1)} collective-permute-done((bf16[8,128,128]{2,1,0:T(8,128)(2,1)S(1)}, bf16[8,128,128]{2,1,0:T(8,128)(2,1)S(1)}, u32[]{:S(2)}, u32[]{:S(2)}) %collective-permute-start.8) | collective-permute-done | bytes 262176 | tf_op jit(solution)/shard_map/ppermute | solution.py:282
  61.7 0.0 copy-done.4
  61.7 0.0 copy-done.5
  61.7 0.9 %faces.1 = (f32[4,32,128]{2,1,0:T(8,128)S(1)}, bf16[4,32,128]{2,1,0:T(8,128)(2,1)S(1)}) custom-call(s32[1,8]{1,0:T(1,128)S(1)} %copy-done.4, s32[8]{0:T(128)S(1)} %copy-done.5, bf16[8,128,128]{2,1,0:T(8,128)(2,1)S(1)} %products.1.mine, bf16[8,128,128]{2,1,0:T(8,128)(2,1)S(1)} %collective-permute-done.8.other), custom_call_target="tpu_custom_call" | custom-call | tf_op jit(solution)/shard_map/faces/pallas_call | solution.py:363
  62.7 3.2 %collective-permute-start.9 = (bf16[4,32,128]{2,1,0:T(8,128)(2,1)S(1)}, bf16[4,32,128]{2,1,0:T(8,128)(2,1)S(1)}, u32[]{:S(2)}, u32[]{:S(2)}) collective-permute-start(bf16[4,32,128]{2,1,0:T(8,128)(2,1)S(1)} %get-tuple-element.10), channel_id=1, source_target_pairs={{0,16},{4,20},{8,24},{12,28},{16,0},{20,4},{24,8},{28,12},{1,17},{... | collective-permute-start | bytes 98312 | tf_op jit(solution)/shard_map/ppermute | solution.py:282
  65.9 1.9 %collective-permute-done.9 = bf16[4,32,128]{2,1,0:T(8,128)(2,1)S(1)} collective-permute-done((bf16[4,32,128]{2,1,0:T(8,128)(2,1)S(1)}, bf16[4,32,128]{2,1,0:T(8,128)(2,1)S(1)}, u32[]{:S(2)}, u32[]{:S(2)}) %collective-permute-start.9) | collective-permute-done | bytes 32800 | tf_op jit(solution)/shard_map/ppermute | solution.py:282
  67.9 1.9 %collective-permute-start.10 = (bf16[2,32,128]{2,1,0:T(8,128)(2,1)S(1)}, bf16[2,32,128]{2,1,0:T(8,128)(2,1)S(1)}, u32[]{:S(2)}, u32[]{:S(2)}) collective-permute-start(bf16[2,32,128]{2,1,0:T(8,128)(2,1)S(1)} %slice.36), channel_id=1, source_target_pairs={{0,8},{4,12},{8,0},{12,4},{16,24},{20,28},{24,16},{28,20},{1,9},{5... | collective-permute-start | bytes 49160 | tf_op jit(solution)/shard_map/ppermute | solution.py:282
  69.8 1.9 %collective-permute-done.10 = bf16[2,32,128]{2,1,0:T(8,128)(2,1)S(1)} collective-permute-done((bf16[2,32,128]{2,1,0:T(8,128)(2,1)S(1)}, bf16[2,32,128]{2,1,0:T(8,128)(2,1)S(1)}, u32[]{:S(2)}, u32[]{:S(2)}) %collective-permute-start.10) | collective-permute-done | bytes 16416 | tf_op jit(solution)/shard_map/ppermute | solution.py:282
  71.7 1.9 %collective-permute-start.11 = (bf16[1,32,128]{2,1,0:T(8,128)(2,1)S(1)}, bf16[1,32,128]{2,1,0:T(8,128)(2,1)S(1)}, u32[]{:S(2)}, u32[]{:S(2)}) collective-permute-start(bf16[1,32,128]{2,1,0:T(8,128)(2,1)S(1)} %slice.37), channel_id=1, source_target_pairs={{0,4},{4,0},{8,12},{12,8},{16,20},{20,16},{24,28},{28,24},{1,5},{5... | collective-permute-start | bytes 24584 | tf_op jit(solution)/shard_map/ppermute | solution.py:282
  73.6 1.8 %collective-permute-done.11 = bf16[1,32,128]{2,1,0:T(8,128)(2,1)S(1)} collective-permute-done((bf16[1,32,128]{2,1,0:T(8,128)(2,1)S(1)}, bf16[1,32,128]{2,1,0:T(8,128)(2,1)S(1)}, u32[]{:S(2)}, u32[]{:S(2)}) %collective-permute-start.11) | collective-permute-done | bytes 8224 | tf_op jit(solution)/shard_map/ppermute | solution.py:282
  75.4 0.6 slice_add_fusion.1
  (6 shorter events, 0.0 us)
Async XLA Ops:
  0.6 6.0 %copy-start = (bf16[1,8,128,512]{3,2,1,0:T(8,128)(2,1)S(1)}, bf16[1,8,128,512]{3,2,1,0:T(8,128)(2,1)}, u32[]{:S(2)}) copy-start(bf16[1,8,128,512]{3,2,1,0:T(8,128)(2,1)} %param.15) | copy-start | bytes 3145732
  0.6 32.8 %collective-permute-start.1 = (bf16[5120,128]{1,0:T(8,128)(2,1)}, bf16[5120,128]{1,0:T(8,128)(2,1)S(1)}, u32[]{:S(2)}, u32[]{:S(2)}) collective-permute-start(bf16[5120,128]{1,0:T(8,128)(2,1)} %bitcast.blocks.k0), channel_id=1, source_target_pairs={{0,2},{1,3},{2,0},{3,1},{4,6},{5,7},{6,4},{7,5},{8,10},{9,11},{10,... | collective-permute-start | bytes 3932168 | tf_op jit(solution)/shard_map/ppermute | solution.py:282
  3.6 0.9 %copy-start.1 = (bf16[1,512,128]{2,1,0:T(8,128)(2,1)S(1)}, bf16[1,512,128]{2,1,0:T(8,128)(2,1)}, u32[]{:S(2)}) copy-start(bf16[1,512,128]{2,1,0:T(8,128)(2,1)} %param.12) | copy-start | bytes 393220
  4.5 0.7 copy-start.2
  5.2 0.7 copy-start.3
  6.1 27.6 %collective-permute-start.4 = (bf16[528,128]{1,0:T(8,128)(2,1)S(1)}, bf16[528,128]{1,0:T(8,128)(2,1)S(1)}, u32[]{:S(2)}, u32[]{:S(2)}) collective-permute-start(bf16[528,128]{1,0:T(8,128)(2,1)S(1)} %pack.1.refs_2_), channel_id=1, source_target_pairs={{0,1},{1,0},{2,3},{3,2},{4,5},{5,4},{6,7},{7,6},{8,9},{9,8},{10,11... | collective-permute-start | bytes 405512 | tf_op jit(solution)/shard_map/ppermute | solution.py:282
  6.2 30.2 %collective-permute-start.5 = (bf16[528,128]{1,0:T(8,128)(2,1)S(1)}, bf16[528,128]{1,0:T(8,128)(2,1)S(1)}, u32[]{:S(2)}, u32[]{:S(2)}) collective-permute-start(bf16[528,128]{1,0:T(8,128)(2,1)S(1)} %pack.1.refs_2_), channel_id=1, source_target_pairs={{0,2},{1,3},{2,0},{3,1},{4,6},{5,7},{6,4},{7,5},{8,10},{9,11},{10,... | collective-permute-start | bytes 405512 | tf_op jit(solution)/shard_map/ppermute | solution.py:282
  6.3 31.4 %collective-permute-start = (bf16[5120,128]{1,0:T(8,128)(2,1)}, bf16[5120,128]{1,0:T(8,128)(2,1)S(1)}, u32[]{:S(2)}, u32[]{:S(2)}) collective-permute-start(bf16[5120,128]{1,0:T(8,128)(2,1)} %bitcast.blocks.k0), channel_id=1, source_target_pairs={{0,1},{1,0},{2,3},{3,2},{4,5},{5,4},{6,7},{7,6},{8,9},{9,8},{10,11... | collective-permute-start | bytes 3932168 | tf_op jit(solution)/shard_map/ppermute | solution.py:282
  6.7 52.3 %collective-permute-start.7 = (bf16[8,128,512]{2,1,0:T(8,128)(2,1)S(1)}, bf16[8,128,512]{2,1,0:T(8,128)(2,1)S(1)}, u32[]{:S(2)}, u32[]{:S(2)}) collective-permute-start(bf16[8,128,512]{2,1,0:T(8,128)(2,1)S(1)} %bitcast.4), channel_id=1, source_target_pairs={{0,2},{1,3},{2,0},{3,1},{4,6},{5,7},{6,4},{7,5},{8,10},{9,11},{10,... | collective-permute-start | bytes 3145736 | tf_op jit(solution)/shard_map/ppermute | solution.py:282
  33.6 4.2 %collective-permute-start.2 = (bf16[2560,128]{1,0:T(8,128)(2,1)S(1)}, bf16[2560,128]{1,0:T(8,128)(2,1)S(1)}, u32[]{:S(2)}, u32[]{:S(2)}) collective-permute-start(bf16[2560,128]{1,0:T(8,128)(2,1)S(1)} %get-tuple-element.13), channel_id=1, source_target_pairs={{0,1},{1,0},{2,3},{3,2},{4,5},{5,4},{6,7},{7,6},{8,9},{9,8},{10,11... | collective-permute-start | bytes 1966088 | tf_op jit(solution)/shard_map/ppermute | solution.py:282
  33.6 4.1 %collective-permute-start.3 = (bf16[2560,128]{1,0:T(8,128)(2,1)S(1)}, bf16[2560,128]{1,0:T(8,128)(2,1)S(1)}, u32[]{:S(2)}, u32[]{:S(2)}) collective-permute-start(bf16[2560,128]{1,0:T(8,128)(2,1)S(1)} %get-tuple-element.12), channel_id=1, source_target_pairs={{0,1},{1,0},{2,3},{3,2},{4,5},{5,4},{6,7},{7,6},{8,9},{9,8},{10,11... | collective-permute-start | bytes 1966088 | tf_op jit(solution)/shard_map/ppermute | solution.py:282
  36.4 1.4 %collective-permute-start.6 = (bf16[528,128]{1,0:T(8,128)(2,1)S(1)}, bf16[528,128]{1,0:T(8,128)(2,1)S(1)}, u32[]{:S(2)}, u32[]{:S(2)}) collective-permute-start(bf16[528,128]{1,0:T(8,128)(2,1)S(1)} %gate.2.refs_4_), channel_id=1, source_target_pairs={{0,1},{1,0},{2,3},{3,2},{4,5},{5,4},{6,7},{7,6},{8,9},{9,8},{10,11... | collective-permute-start | bytes 405512 | tf_op jit(solution)/shard_map/ppermute | solution.py:282
  59.0 2.7 %copy-start.4 = (s32[1,8]{1,0:T(1,128)S(1)}, s32[1,8]{1,0:T(1,128)}, u32[]{:S(2)}) copy-start(s32[1,8]{1,0:T(1,128)} %links.1) | copy-start | bytes 100
  59.0 2.7 %copy-start.5 = (s32[8]{0:T(128)S(1)}, s32[8]{0:T(128)}, u32[]{:S(2)}) copy-start(s32[8]{0:T(128)} %slots.1) | copy-start | bytes 100
  60.0 1.7 %collective-permute-start.8 = (bf16[8,128,128]{2,1,0:T(8,128)(2,1)S(1)}, bf16[8,128,128]{2,1,0:T(8,128)(2,1)S(1)}, u32[]{:S(2)}, u32[]{:S(2)}) collective-permute-start(bf16[8,128,128]{2,1,0:T(8,128)(2,1)S(1)} %products.1.mine), channel_id=1, source_target_pairs={{0,1},{1,0},{2,3},{3,2},{4,5},{5,4},{6,7},{7,6},{8,9},{9,8},{10,11... | collective-permute-start | bytes 786440 | tf_op jit(solution)/shard_map/ppermute | solution.py:282
  62.7 5.2 %collective-permute-start.9 = (bf16[4,32,128]{2,1,0:T(8,128)(2,1)S(1)}, bf16[4,32,128]{2,1,0:T(8,128)(2,1)S(1)}, u32[]{:S(2)}, u32[]{:S(2)}) collective-permute-start(bf16[4,32,128]{2,1,0:T(8,128)(2,1)S(1)} %get-tuple-element.10), channel_id=1, source_target_pairs={{0,16},{4,20},{8,24},{12,28},{16,0},{20,4},{24,8},{28,12},{1,17},{... | collective-permute-start | bytes 98312 | tf_op jit(solution)/shard_map/ppermute | solution.py:282
  67.9 3.8 %collective-permute-start.10 = (bf16[2,32,128]{2,1,0:T(8,128)(2,1)S(1)}, bf16[2,32,128]{2,1,0:T(8,128)(2,1)S(1)}, u32[]{:S(2)}, u32[]{:S(2)}) collective-permute-start(bf16[2,32,128]{2,1,0:T(8,128)(2,1)S(1)} %slice.36), channel_id=1, source_target_pairs={{0,8},{4,12},{8,0},{12,4},{16,24},{20,28},{24,16},{28,20},{1,9},{5... | collective-permute-start | bytes 49160 | tf_op jit(solution)/shard_map/ppermute | solution.py:282
  71.7 3.7 %collective-permute-start.11 = (bf16[1,32,128]{2,1,0:T(8,128)(2,1)S(1)}, bf16[1,32,128]{2,1,0:T(8,128)(2,1)S(1)}, u32[]{:S(2)}, u32[]{:S(2)}) collective-permute-start(bf16[1,32,128]{2,1,0:T(8,128)(2,1)S(1)} %slice.37), channel_id=1, source_target_pairs={{0,4},{4,0},{8,12},{12,8},{16,20},{20,16},{24,28},{28,24},{1,5},{5... | collective-permute-start | bytes 24584 | tf_op jit(solution)/shard_map/ppermute | solution.py:282

commit v5 on v4

--- a/solution.py
+++ b/solution.py
@@ -33,7 +33,7 @@
     return jnp.concatenate([p.astype(F32) for p in parts], axis=0).astype(BF16)
 
 
-def inverse_factor(gram, between, near=3):
+def inverse_factor(gram, between, near=2):
     n = gram.shape[0]
     lane = lax.broadcasted_iota(jnp.int32, (8, n), 1)
     sub = lax.broadcasted_iota(jnp.int32, (8, n), 0)
@@ -126,10 +126,11 @@
     k3, refs = refs[:SPLIT], refs[SPLIT:]
     (
         a0, a1, a2, a3, phi_out, theta_out, rs_out,
-        ya, yb, zs, scale, heavy, codes, pat, mine, psem, ksem,
+        yb, zs, scale, heavy, codes, pat, mine, psem, ksem,
     ) = refs
     fetch = pltpu.make_async_copy(k0, mine, ksem.at[0])
     fetch.start()
+    ya = phi_out
     bs = k0.shape[1]
     nb = own * nranks
     held = own * bs
@@ -139,28 +140,17 @@
     def rows_of(i):
         return pl.ds(i * bs if isinstance(i, int) else pl.multiple_of(i * bs, bs), bs)
 
-    mass = [None] * nb
-    lines = a0.shape[0] - held
-    smalls = [ref[held:, :].astype(F32) for ref in (a0, a1, a2, a3)]
-    for r in range(nranks):
-        rows = smalls[0]
-        for t in range(1, nranks):
-            rows = jnp.where((me ^ t) == r, smalls[t], rows)
-        rows = jnp.where(me == r, smalls[0], rows)
-        codes[r * own : (r + 1) * own, :] = rows[3 * own : 4 * own, :].astype(jnp.int32)
-        whole = rows[:own] + rows[own : 2 * own] + rows[2 * own : 3 * own]
-        for i in range(own):
-            mass[r * own + i] = whole[i : i + 1, :]
+    mass = []
+    for t, ref in enumerate((a0, a1, a2, a3)):
+        rows = ref[held:, :].astype(F32)
+        codes[t * own : (t + 1) * own, :] = rows[3 * own : 4 * own, :].astype(jnp.int32)
+        mass.append(rows[:own] + rows[own : 2 * own] + rows[2 * own : 3 * own])
     down = pltpu.make_async_copy(codes, pat, psem.at[0])
     down.start()
     for t, ref in enumerate((a0, a1, a2, a3)):
         ya[pl.ds(pl.multiple_of((me ^ t) * held, held), held), :] = ref[:held, :]
     centre = (high[0] + low[0]) / 2.0
     half = (high[0] - low[0]) / 2.0
-    for i in range(nb):
-        row = jnp.broadcast_to(mass[i], (bs, bs)).T
-        heavy[i * bs : (i + 1) * bs, :] = row
-        scale[i * bs : (i + 1) * bs, :] = 1.0 / (row * half)
     shift = jnp.full((1, 1), centre, F32) / half
     down.wait()
 
@@ -169,21 +159,25 @@
             for r in range(own):
                 yield t, r, (me ^ t) * own + r
 
-    def image(t, r, i, src):
+    def image(t, r, src):
         if t < 3:
             left = [kept[t][rows_of(r * nzb + k), :] for k in range(nzb)]
         else:
             per = own // SPLIT
             left = [k3[r // per][rows_of(r % per * nzb + k), :] for k in range(nzb)]
         left = jnp.concatenate(left, axis=1)
-        right = jnp.concatenate([src[rows_of(pat[i, k]), :] for k in range(nzb)], axis=0)
+        right = jnp.concatenate([src[rows_of(pat[t * own + r, k]), :] for k in range(nzb)], axis=0)
         return jnp.dot(left, right, preferred_element_type=F32)
 
     for t, r, i in sorted(order(), key=lambda x: x[0] == 0):
         if (t, r) == (0, 0):
             fetch.wait()
         at = rows_of(i)
-        yb[at, :] = (image(t, r, i, ya) * scale[at, :] - shift * ya[at, :].astype(F32)).astype(BF16)
+        row = jnp.broadcast_to(mass[t][r : r + 1, :], (bs, bs)).T
+        heavy[at, :] = row
+        scaled = 1.0 / (row * half)
+        scale[at, :] = scaled
+        yb[at, :] = (image(t, r, ya) * scaled - shift * ya[at, :].astype(F32)).astype(BF16)
 
     @pl.loop(0, ITERS)
     def _(it):
@@ -192,7 +186,7 @@
             for t, r, i in order():
                 at = rows_of(i)
                 dst[at, :] = (
-                    2.0 * (image(t, r, i, src) * scale[at, :] - shift * src[at, :].astype(F32))
+                    2.0 * (image(t, r, src) * scale[at, :] - shift * src[at, :].astype(F32))
                     - dst[at, :].astype(F32)
                 ).astype(BF16)
             src, dst = dst, src
@@ -209,7 +203,7 @@
 
         def between(b):
             for t, r, i in todo[nb * b // groups : nb * (b + 1) // groups]:
-                zs[rows_of(i), :] = image(t, r, i, cur).astype(BF16)
+                zs[rows_of(i), :] = image(t, r, cur).astype(BF16)
 
         groups = bs // 8
         hi, lo = split2(inverse_factor(gram, between))
@@ -229,23 +223,17 @@
         theta_out[...] = theta
         rs_out[...] = jnp.broadcast_to(lax.rsqrt(theta), rs_out.shape)
 
-    phi_out[...] = ya[...]
-
-
-def product_kernel(phi, rs, c0, c2, out, held, sem):
+
+def product_kernel(phi, rs, c0, c2, out):
     me = lax.axis_index("split")
     njs, bs, cols = c0.shape
-    copies = []
-    for t, ref in enumerate((c0, c2)):
-        copies.append(pltpu.make_async_copy(ref, held.at[t], sem.at[t]))
-        copies[-1].start()
-    prods = None
-    for t, c in enumerate(copies):
-        c.wait()
-        at = pl.multiple_of((me ^ (2 * t)) * cols, cols)
-        part = jnp.dot(held[t].reshape(njs * bs, cols), phi[pl.ds(at, cols), :], preferred_element_type=F32)
-        prods = part if prods is None else prods + part
-    out[...] = (prods * rs[0:1, :]).astype(BF16).reshape(out.shape)
+    mine = phi[pl.ds(pl.multiple_of(me * cols, cols), cols), :]
+    other = phi[pl.ds(pl.multiple_of((me ^ 2) * cols, cols), cols), :]
+    right = jnp.concatenate([mine, other], axis=0)
+    scale = rs[0:1, :]
+    for j in range(njs):
+        left = jnp.concatenate([c0[j], c2[j]], axis=1)
+        out[j] = (jnp.dot(left, right, preferred_element_type=F32) * scale).astype(BF16)
 
 
 def face_kernel(nranks, nsub, links, slots, mine, other, keep, send, dense):
@@ -335,7 +323,6 @@
         scratch_shapes=[
             pltpu.VMEM((nb * bs, modes), BF16),
             pltpu.VMEM((nb * bs, modes), BF16),
-            pltpu.VMEM((nb * bs, modes), BF16),
             pltpu.VMEM((nb * bs, modes), F32),
             pltpu.VMEM((nb * bs, modes), F32),
             pltpu.VMEM((nb, modes), jnp.int32),
@@ -350,13 +337,12 @@
     )(cut_low, cut_high, blocks, k_1, k_2, *k_3, a_0, a_1, a_2, a_3)
 
     share = bs // nranks
-    nif, _, cols = coupling.shape[1:]
+    nif = coupling.shape[1]
     prods = pl.pallas_call(
         product_kernel,
         out_shape=jax.ShapeDtypeStruct((nif, bs, modes), BF16),
-        in_specs=[vmem, vmem, hbm, hbm],
+        in_specs=[vmem] * 4,
         out_specs=vmem,
-        scratch_shapes=[pltpu.VMEM((2, nif, bs, cols), BF16), pltpu.SemaphoreType.DMA((2,))],
         compiler_params=pltpu.CompilerParams(vmem_limit_bytes=16 << 20),
         name="products",
     )(phi, rs, coupling[0], c_2)

time: 76.2 us -> 75.8 us (level)
  no operation moved by 1% of the time
where the time goes in v5:
time: 75.8 us; the launch traced here: 75.6 us
  waiting for transfers between devices  34.1 us (45%)
  Pallas kernels  23 us (30%)
  starting transfers between devices  13.5 us (18%)
  local copies, waits for them, and re-layouts  2.38 us (3%)
  between operations  2.05 us (3%)
    ppermute x12, waiting for transfers between devices, swap(): return lax.ppermute(x, axis, [(i, i ^ bits) for i in range(n)])  34.1 us
    pallas_call x1, Pallas kernels, shards(): pl.pallas_call(functools.partial(filter_kernel, nranks, own, nzb), out_sh...  21.1 us
    ppermute x12, starting transfers between devices, swap(): return lax.ppermute(x, axis, [(i, i ^ bits) for i in range(n)])  13.5 us
    unnamed x12, local copies, waits for them, and re-layouts  2.28 us
  transfers between devices with their start and end apart: 12, of which 7 were waited for; matrix products, arithmetic and copies ran while one was open for 0% of the time, Pallas kernels for 28%

profile of v5, /device:TPU:0, one launch (start us, length us, event | category | flops | bytes accessed | tf_op | source)
XLA Modules:
  0.0 75.6 jit_solution(6856331657557816903)
XLA Ops:
  0.6 0.0 copy-start
  0.6 3.0 %collective-permute-start.1 = (bf16[5120,128]{1,0:T(8,128)(2,1)}, bf16[5120,128]{1,0:T(8,128)(2,1)S(1)}, u32[]{:S(2)}, u32[]{:S(2)}) collective-permute-start(bf16[5120,128]{1,0:T(8,128)(2,1)} %bitcast.blocks.k0), channel_id=1, source_target_pairs={{0,2},{1,3},{2,0},{3,1},{4,6},{5,7},{6,4},{7,5},{8,10},{9,11},{10,... | collective-permute-start | bytes 3932168 | tf_op jit(solution)/shard_map/ppermute | solution.py:270
  3.6 0.0 copy-start.1
  3.6 0.9 %copy-done.1 = bf16[1,512,128]{2,1,0:T(8,128)(2,1)S(1)} copy-done((bf16[1,512,128]{2,1,0:T(8,128)(2,1)S(1)}, bf16[1,512,128]{2,1,0:T(8,128)(2,1)}, u32[]{:S(2)}) %copy-start.1) | copy-done | bytes 131096
  4.5 0.0 copy-start.2
  4.6 0.7 copy-done.2
  5.2 0.0 copy-start.3
  5.2 0.7 copy-done.3
  5.9 0.2 pack.1.refs_2_
  6.1 0.1 collective-permute-start.4
  6.2 0.2 collective-permute-start.5
  6.3 0.3 collective-permute-start
  6.7 0.0 copy-done
  6.7 1.8 %collective-permute-start.7 = (bf16[8,128,512]{2,1,0:T(8,128)(2,1)S(1)}, bf16[8,128,512]{2,1,0:T(8,128)(2,1)S(1)}, u32[]{:S(2)}, u32[]{:S(2)}) collective-permute-start(bf16[8,128,512]{2,1,0:T(8,128)(2,1)S(1)} %bitcast.4), channel_id=1, source_target_pairs={{0,2},{1,3},{2,0},{3,1},{4,6},{5,7},{6,4},{7,5},{8,10},{9,11},{10,... | collective-permute-start | bytes 3145736 | tf_op jit(solution)/shard_map/ppermute | solution.py:270
  8.4 25.0 %collective-permute-done.1.k2 = bf16[5120,128]{1,0:T(8,128)(2,1)S(1)} collective-permute-done((bf16[5120,128]{1,0:T(8,128)(2,1)}, bf16[5120,128]{1,0:T(8,128)(2,1)S(1)}, u32[]{:S(2)}, u32[]{:S(2)}) %collective-permute-start.1) | collective-permute-done | bytes 1310752 | tf_op jit(solution)/shard_map/ppermute | solution.py:270
  33.5 0.1 fusion
  33.6 0.1 collective-permute-start.2
  33.6 0.0 collective-permute-done.4.refs_1_.refs_3_
  33.6 0.5 collective-permute-start.3
  34.1 2.2 %collective-permute-done.5.refs_0_ = bf16[528,128]{1,0:T(8,128)(2,1)S(1)} collective-permute-done((bf16[528,128]{1,0:T(8,128)(2,1)S(1)}, bf16[528,128]{1,0:T(8,128)(2,1)S(1)}, u32[]{:S(2)}, u32[]{:S(2)}) %collective-permute-start.5) | collective-permute-done | bytes 135200 | tf_op jit(solution)/shard_map/ppermute | solution.py:270
  36.4 0.0 collective-permute-start.6
  37.7 0.1 collective-permute-done.6.refs_0_
  37.7 0.0 collective-permute-done.k1
  37.7 0.0 collective-permute-done.2.refs_0_
  37.7 0.0 collective-permute-done.3.refs_1_
  37.7 21.1 %filter.1 = (bf16[2048,128]{1,0:T(8,128)(2,1)S(1)}, f32[1,128]{1,0:T(1,128)}, f32[8,128]{1,0:T(8,128)S(1)}) custom-call(f32[1]{0:T(128)S(6)} %copy.15.low, f32[1]{0:T(128)S(6)} %copy.16.high, bf16[5120,128]{1,0:T(8,128)(2,1)} %bitcast.blocks.k0, bf16[5120,128]{1,0:T(8,128)(2,1)S(1)} %collective-permute-done.k1, ...), custom_call_target="tpu_custom_call" | custom-call | flops 1000000000 | bytes 8388608 | tf_op jit(solution)/shard_map/filter/pallas_call | solution.py:314
  58.9 0.0 collective-permute-done.7.c2
  58.9 0.0 copy-start.4
  58.9 0.0 copy-start.5
  58.9 0.7 products.1.mine
  59.6 0.6 collective-permute-start.8
  60.2 1.2 %collective-permute-done.8.other = bf16[8,128,128]{2,1,0:T(8,128)(2,1)S(1)} collective-permute-done((bf16[8,128,128]{2,1,0:T(8,128)(2,1)S(1)}, bf16[8,128,128]{2,1,0:T(8,128)(2,1)S(1)}, u32[]{:S(2)}, u32[]{:S(2)}) %collective-permute-start.8) | collective-permute-done | bytes 262176 | tf_op jit(solution)/shard_map/ppermute | solution.py:270
  61.4 0.0 copy-done.4
  61.4 0.0 copy-done.5
  61.4 0.9 %faces.1 = (f32[4,32,128]{2,1,0:T(8,128)S(1)}, bf16[4,32,128]{2,1,0:T(8,128)(2,1)S(1)}) custom-call(s32[1,8]{1,0:T(1,128)S(1)} %copy-done.4, s32[8]{0:T(128)S(1)} %copy-done.5, bf16[8,128,128]{2,1,0:T(8,128)(2,1)S(1)} %products.1.mine, bf16[8,128,128]{2,1,0:T(8,128)(2,1)S(1)} %collective-permute-done.8.other), custom_call_target="tpu_custom_call" | custom-call | tf_op jit(solution)/shard_map/faces/pallas_call | solution.py:349
  62.3 3.2 %collective-permute-start.9 = (bf16[4,32,128]{2,1,0:T(8,128)(2,1)S(1)}, bf16[4,32,128]{2,1,0:T(8,128)(2,1)S(1)}, u32[]{:S(2)}, u32[]{:S(2)}) collective-permute-start(bf16[4,32,128]{2,1,0:T(8,128)(2,1)S(1)} %get-tuple-element.10), channel_id=1, source_target_pairs={{0,16},{4,20},{8,24},{12,28},{16,0},{20,4},{24,8},{28,12},{1,17},{... | collective-permute-start | bytes 98312 | tf_op jit(solution)/shard_map/ppermute | solution.py:270
  65.5 1.9 %collective-permute-done.9 = bf16[4,32,128]{2,1,0:T(8,128)(2,1)S(1)} collective-permute-done((bf16[4,32,128]{2,1,0:T(8,128)(2,1)S(1)}, bf16[4,32,128]{2,1,0:T(8,128)(2,1)S(1)}, u32[]{:S(2)}, u32[]{:S(2)}) %collective-permute-start.9) | collective-permute-done | bytes 32800 | tf_op jit(solution)/shard_map/ppermute | solution.py:270
  67.5 1.9 %collective-permute-start.10 = (bf16[2,32,128]{2,1,0:T(8,128)(2,1)S(1)}, bf16[2,32,128]{2,1,0:T(8,128)(2,1)S(1)}, u32[]{:S(2)}, u32[]{:S(2)}) collective-permute-start(bf16[2,32,128]{2,1,0:T(8,128)(2,1)S(1)} %slice.36), channel_id=1, source_target_pairs={{0,8},{4,12},{8,0},{12,4},{16,24},{20,28},{24,16},{28,20},{1,9},{5... | collective-permute-start | bytes 49160 | tf_op jit(solution)/shard_map/ppermute | solution.py:270
  69.4 1.9 %collective-permute-done.10 = bf16[2,32,128]{2,1,0:T(8,128)(2,1)S(1)} collective-permute-done((bf16[2,32,128]{2,1,0:T(8,128)(2,1)S(1)}, bf16[2,32,128]{2,1,0:T(8,128)(2,1)S(1)}, u32[]{:S(2)}, u32[]{:S(2)}) %collective-permute-start.10) | collective-permute-done | bytes 16416 | tf_op jit(solution)/shard_map/ppermute | solution.py:270
  71.3 1.9 %collective-permute-start.11 = (bf16[1,32,128]{2,1,0:T(8,128)(2,1)S(1)}, bf16[1,32,128]{2,1,0:T(8,128)(2,1)S(1)}, u32[]{:S(2)}, u32[]{:S(2)}) collective-permute-start(bf16[1,32,128]{2,1,0:T(8,128)(2,1)S(1)} %slice.37), channel_id=1, source_target_pairs={{0,4},{4,0},{8,12},{12,8},{16,20},{20,16},{24,28},{28,24},{1,5},{5... | collective-permute-start | bytes 24584 | tf_op jit(solution)/shard_map/ppermute | solution.py:270
  73.2 1.8 %collective-permute-done.11 = bf16[1,32,128]{2,1,0:T(8,128)(2,1)S(1)} collective-permute-done((bf16[1,32,128]{2,1,0:T(8,128)(2,1)S(1)}, bf16[1,32,128]{2,1,0:T(8,128)(2,1)S(1)}, u32[]{:S(2)}, u32[]{:S(2)}) %collective-permute-start.11) | collective-permute-done | bytes 8224 | tf_op jit(solution)/shard_map/ppermute | solution.py:270
  75.0 0.6 slice_add_fusion.1
  (6 shorter events, 0.0 us)
Async XLA Ops:
  0.6 6.0 %copy-start = (bf16[1,8,128,512]{3,2,1,0:T(8,128)(2,1)S(1)}, bf16[1,8,128,512]{3,2,1,0:T(8,128)(2,1)}, u32[]{:S(2)}) copy-start(bf16[1,8,128,512]{3,2,1,0:T(8,128)(2,1)} %param.15) | copy-start | bytes 3145732
  0.6 32.8 %collective-permute-start.1 = (bf16[5120,128]{1,0:T(8,128)(2,1)}, bf16[5120,128]{1,0:T(8,128)(2,1)S(1)}, u32[]{:S(2)}, u32[]{:S(2)}) collective-permute-start(bf16[5120,128]{1,0:T(8,128)(2,1)} %bitcast.blocks.k0), channel_id=1, source_target_pairs={{0,2},{1,3},{2,0},{3,1},{4,6},{5,7},{6,4},{7,5},{8,10},{9,11},{10,... | collective-permute-start | bytes 3932168 | tf_op jit(solution)/shard_map/ppermute | solution.py:270
  3.6 0.9 %copy-start.1 = (bf16[1,512,128]{2,1,0:T(8,128)(2,1)S(1)}, bf16[1,512,128]{2,1,0:T(8,128)(2,1)}, u32[]{:S(2)}) copy-start(bf16[1,512,128]{2,1,0:T(8,128)(2,1)} %param.12) | copy-start | bytes 393220
  4.5 0.7 copy-start.2
  5.2 0.7 copy-start.3
  6.1 27.6 %collective-permute-start.4 = (bf16[528,128]{1,0:T(8,128)(2,1)S(1)}, bf16[528,128]{1,0:T(8,128)(2,1)S(1)}, u32[]{:S(2)}, u32[]{:S(2)}) collective-permute-start(bf16[528,128]{1,0:T(8,128)(2,1)S(1)} %pack.1.refs_2_), channel_id=1, source_target_pairs={{0,1},{1,0},{2,3},{3,2},{4,5},{5,4},{6,7},{7,6},{8,9},{9,8},{10,11... | collective-permute-start | bytes 405512 | tf_op jit(solution)/shard_map/ppermute | solution.py:270
  6.2 30.2 %collective-permute-start.5 = (bf16[528,128]{1,0:T(8,128)(2,1)S(1)}, bf16[528,128]{1,0:T(8,128)(2,1)S(1)}, u32[]{:S(2)}, u32[]{:S(2)}) collective-permute-start(bf16[528,128]{1,0:T(8,128)(2,1)S(1)} %pack.1.refs_2_), channel_id=1, source_target_pairs={{0,2},{1,3},{2,0},{3,1},{4,6},{5,7},{6,4},{7,5},{8,10},{9,11},{10,... | collective-permute-start | bytes 405512 | tf_op jit(solution)/shard_map/ppermute | solution.py:270
  6.3 31.4 %collective-permute-start = (bf16[5120,128]{1,0:T(8,128)(2,1)}, bf16[5120,128]{1,0:T(8,128)(2,1)S(1)}, u32[]{:S(2)}, u32[]{:S(2)}) collective-permute-start(bf16[5120,128]{1,0:T(8,128)(2,1)} %bitcast.blocks.k0), channel_id=1, source_target_pairs={{0,1},{1,0},{2,3},{3,2},{4,5},{5,4},{6,7},{7,6},{8,9},{9,8},{10,11... | collective-permute-start | bytes 3932168 | tf_op jit(solution)/shard_map/ppermute | solution.py:270
  6.7 52.2 %collective-permute-start.7 = (bf16[8,128,512]{2,1,0:T(8,128)(2,1)S(1)}, bf16[8,128,512]{2,1,0:T(8,128)(2,1)S(1)}, u32[]{:S(2)}, u32[]{:S(2)}) collective-permute-start(bf16[8,128,512]{2,1,0:T(8,128)(2,1)S(1)} %bitcast.4), channel_id=1, source_target_pairs={{0,2},{1,3},{2,0},{3,1},{4,6},{5,7},{6,4},{7,5},{8,10},{9,11},{10,... | collective-permute-start | bytes 3145736 | tf_op jit(solution)/shard_map/ppermute | solution.py:270
  33.6 4.2 %collective-permute-start.2 = (bf16[2560,128]{1,0:T(8,128)(2,1)S(1)}, bf16[2560,128]{1,0:T(8,128)(2,1)S(1)}, u32[]{:S(2)}, u32[]{:S(2)}) collective-permute-start(bf16[2560,128]{1,0:T(8,128)(2,1)S(1)} %get-tuple-element.13), channel_id=1, source_target_pairs={{0,1},{1,0},{2,3},{3,2},{4,5},{5,4},{6,7},{7,6},{8,9},{9,8},{10,11... | collective-permute-start | bytes 1966088 | tf_op jit(solution)/shard_map/ppermute | solution.py:270
  33.6 4.1 %collective-permute-start.3 = (bf16[2560,128]{1,0:T(8,128)(2,1)S(1)}, bf16[2560,128]{1,0:T(8,128)(2,1)S(1)}, u32[]{:S(2)}, u32[]{:S(2)}) collective-permute-start(bf16[2560,128]{1,0:T(8,128)(2,1)S(1)} %get-tuple-element.12), channel_id=1, source_target_pairs={{0,1},{1,0},{2,3},{3,2},{4,5},{5,4},{6,7},{7,6},{8,9},{9,8},{10,11... | collective-permute-start | bytes 1966088 | tf_op jit(solution)/shard_map/ppermute | solution.py:270
  36.4 1.4 %collective-permute-start.6 = (bf16[528,128]{1,0:T(8,128)(2,1)S(1)}, bf16[528,128]{1,0:T(8,128)(2,1)S(1)}, u32[]{:S(2)}, u32[]{:S(2)}) collective-permute-start(bf16[528,128]{1,0:T(8,128)(2,1)S(1)} %gate.2.refs_4_), channel_id=1, source_target_pairs={{0,1},{1,0},{2,3},{3,2},{4,5},{5,4},{6,7},{7,6},{8,9},{9,8},{10,11... | collective-permute-start | bytes 405512 | tf_op jit(solution)/shard_map/ppermute | solution.py:270
  58.9 2.5 %copy-start.4 = (s32[1,8]{1,0:T(1,128)S(1)}, s32[1,8]{1,0:T(1,128)}, u32[]{:S(2)}) copy-start(s32[1,8]{1,0:T(1,128)} %links.1) | copy-start | bytes 100
  58.9 2.5 %copy-start.5 = (s32[8]{0:T(128)S(1)}, s32[8]{0:T(128)}, u32[]{:S(2)}) copy-start(s32[8]{0:T(128)} %slots.1) | copy-start | bytes 100
  59.6 1.7 %collective-permute-start.8 = (bf16[8,128,128]{2,1,0:T(8,128)(2,1)S(1)}, bf16[8,128,128]{2,1,0:T(8,128)(2,1)S(1)}, u32[]{:S(2)}, u32[]{:S(2)}) collective-permute-start(bf16[8,128,128]{2,1,0:T(8,128)(2,1)S(1)} %products.1.mine), channel_id=1, source_target_pairs={{0,1},{1,0},{2,3},{3,2},{4,5},{5,4},{6,7},{7,6},{8,9},{9,8},{10,11... | collective-permute-start | bytes 786440 | tf_op jit(solution)/shard_map/ppermute | solution.py:270
  62.3 5.2 %collective-permute-start.9 = (bf16[4,32,128]{2,1,0:T(8,128)(2,1)S(1)}, bf16[4,32,128]{2,1,0:T(8,128)(2,1)S(1)}, u32[]{:S(2)}, u32[]{:S(2)}) collective-permute-start(bf16[4,32,128]{2,1,0:T(8,128)(2,1)S(1)} %get-tuple-element.10), channel_id=1, source_target_pairs={{0,16},{4,20},{8,24},{12,28},{16,0},{20,4},{24,8},{28,12},{1,17},{... | collective-permute-start | bytes 98312 | tf_op jit(solution)/shard_map/ppermute | solution.py:270
  67.5 3.8 %collective-permute-start.10 = (bf16[2,32,128]{2,1,0:T(8,128)(2,1)S(1)}, bf16[2,32,128]{2,1,0:T(8,128)(2,1)S(1)}, u32[]{:S(2)}, u32[]{:S(2)}) collective-permute-start(bf16[2,32,128]{2,1,0:T(8,128)(2,1)S(1)} %slice.36), channel_id=1, source_target_pairs={{0,8},{4,12},{8,0},{12,4},{16,24},{20,28},{24,16},{28,20},{1,9},{5... | collective-permute-start | bytes 49160 | tf_op jit(solution)/shard_map/ppermute | solution.py:270
  71.3 3.7 %collective-permute-start.11 = (bf16[1,32,128]{2,1,0:T(8,128)(2,1)S(1)}, bf16[1,32,128]{2,1,0:T(8,128)(2,1)S(1)}, u32[]{:S(2)}, u32[]{:S(2)}) collective-permute-start(bf16[1,32,128]{2,1,0:T(8,128)(2,1)S(1)} %slice.37), channel_id=1, source_target_pairs={{0,4},{4,0},{8,12},{12,8},{16,20},{20,16},{24,28},{28,24},{1,5},{5... | collective-permute-start | bytes 24584 | tf_op jit(solution)/shard_map/ppermute | solution.py:270
